TPU v7x, 256 devices: a whole 4x4x8 slice. The times are simulated.
256 devices in a mesh: pts: 64 (over y, z_lo, x), prb: 4 (over z_hi, core).
Axes of the slice: x: 4, y: 4, z: 8 (z_hi: 2, z_lo: 4; z = z_hi * 4 + z_lo), core: 2. Of those that a mesh axis runs over, the one named last changes fastest.
Arguments:
- probe_vectors: bfloat16 [2, 32, 524288], P(None, 'prb', 'pts'), may hold values from -6 to 6
- factors: bfloat16 [6, 2, 524288, 128], P(None, None, ('pts', 'prb')), may hold values from -0.375 to 0.375
- row_orders: int32 [6, 2048], replicated, may hold values from 0 to 2047, each once within a row
Outputs:
- applied: bfloat16 [2, 32, 524288], P(None, 'prb', 'pts')
All inputs are finite; a program needn't handle non-finite values.
Results may differ from a plain program's by a relative error of at most 0.013.
Values may be sent and summed in bfloat16 or wider, within the bound.
No kernel may reach another device: no remote copies, remote signals or barrier semaphores. Data moves between devices by JAX's collectives and lax.ppermute only.
A program may use at most 128 MiB of HBM per device.

v0:
```python
import jax
import jax.numpy as jnp
from jax import lax
from jax.sharding import PartitionSpec as P

RANK = 64
LEVELS = 6


def from_partner(value, axis, apart):
    return lax.ppermute(value, axis, [(i, i ^ 1 << apart) for i in range(lax.axis_size(axis))])


def permute_rows(current, order_row):
    shape = current.shape
    rows = shape[-1]
    flat = current.reshape(-1, rows)
    width = min(rows, 512)
    count = rows // width
    sources = jnp.arange(rows, dtype=jnp.int32)

    def one_block(targets):
        selector = (sources[:, None] == targets[None, :]).astype(jnp.bfloat16)
        return jnp.dot(flat, selector, preferred_element_type=jnp.float32)

    pieces = lax.map(one_block, order_row.reshape(count, width))
    joined = jnp.transpose(pieces, (1, 0, 2)).reshape(shape)
    return joined.astype(jnp.bfloat16)


def butterfly_level(current, order_row, layer_weights, bit):
    probes_here = current.shape[1]
    groups = current.shape[2]
    rows = current.shape[3]
    half_rows = rows // 2
    block = 2 * RANK
    nblocks = rows // block
    permuted = permute_rows(current, order_row)
    upper_half = lax.axis_index("pts") // (1 << bit) % 2
    kept_rows = lax.dynamic_slice_in_dim(permuted, upper_half * half_rows, half_rows, 3)
    send_rows = lax.dynamic_slice_in_dim(permuted, (1 - upper_half) * half_rows, half_rows, 3)
    got_rows = from_partner(send_rows, "pts", bit)
    joined = jnp.concatenate(
        [
            kept_rows.reshape(2, probes_here, groups, nblocks, RANK),
            got_rows.reshape(2, probes_here, groups, nblocks, RANK),
        ],
        axis=4,
    )
    blocks = layer_weights.reshape(2, groups, nblocks, block, block)
    real_part = jnp.einsum(
        "pgki,gkoi->pgko", joined[0], blocks[0], preferred_element_type=jnp.float32
    ) - jnp.einsum("pgki,gkoi->pgko", joined[1], blocks[1], preferred_element_type=jnp.float32)
    imag_part = jnp.einsum(
        "pgki,gkoi->pgko", joined[1], blocks[0], preferred_element_type=jnp.float32
    ) + jnp.einsum("pgki,gkoi->pgko", joined[0], blocks[1], preferred_element_type=jnp.float32)
    return (
        jnp.stack([real_part, imag_part]).reshape(2, probes_here, groups, rows).astype(jnp.bfloat16)
    )


def local(probe_vectors, factors, row_orders):
    pts_count = lax.axis_size("pts")
    prb_count = lax.axis_size("prb")
    bit_count = pts_count.bit_length() - 1
    rows = factors.shape[2]
    piece_rows = rows // pts_count
    current = lax.all_to_all(probe_vectors, "prb", split_axis=2, concat_axis=1, tiled=True)
    current = current[:, :, None, :]
    for level_index in range(LEVELS):
        layer_weights = factors[level_index]
        current = butterfly_level(
            current, row_orders[level_index], layer_weights, level_index % bit_count
        )
    outgoing = current.reshape(2, current.shape[1], 1, pts_count, piece_rows)
    arrived = lax.all_to_all(
        lax.all_to_all(outgoing, "pts", split_axis=3, concat_axis=3, tiled=True),
        "prb",
        split_axis=1,
        concat_axis=2,
        tiled=True,
    )
    ordered = jnp.transpose(arrived, (0, 1, 4, 2, 3))
    return ordered.reshape(2, arrived.shape[1], piece_rows * prb_count * pts_count)


def solution(mesh):
    placed = (P(None, "prb", "pts"), P(None, None, ("pts", "prb"), None), P())
    return jax.shard_map(
        local, mesh=mesh, in_specs=placed, out_specs=P(None, "prb", "pts"), check_vma=False
    )
```

profile of v0, /device:TPU:32, one launch (start us, length us, event | category | flops | bytes accessed | tf_op | source)
XLA Modules:
  0.0 181.7 jit_solution(10784014017718057980)
XLA Ops:
  0.0 8.3 %copy.67 = bf16[2,8,8192]{1,0,2:T(2,128)(2,1)} copy(bf16[2,8,8192]{2,1,0:T(8,128)(2,1)} %param.15) | data formatting | bytes 524288 | tf_op args[0]
  8.3 6.4 %reshape.540 = bf16[4,2,16384]{2,1,0:T(2,128)(2,1)} reshape(bf16[8192,2,8]{2,1,0:T(2,128)(2,1)} %bitcast.377) | data formatting | bytes 524288
  14.8 7.6 %all-to-all-start = ((bf16[4,2,16384]{2,1,0:T(2,128)(2,1)}), bf16[4,2,16384]{2,1,0:T(2,128)(2,1)S(1)}, u32[]{:S(2)}, u32[]{:S(2)}) async-start(bf16[4,2,16384]{2,1,0:T(2,128)(2,1)} %reshape.540), calls=%async_computation | async-start | bytes 524288 | tf_op jit(solution)/shard_map/all_to_all | solution.py:68
  23.0 12.1 %all-to-all-done = bf16[4,2,16384]{2,1,0:T(2,128)(2,1)S(1)} async-done(((bf16[4,2,16384]{2,1,0:T(2,128)(2,1)}), bf16[4,2,16384]{2,1,0:T(2,128)(2,1)S(1)}, u32[]{:S(2)}, u32[]{:S(2)}) %all-to-all-start) | async-done | bytes 262176 | tf_op jit(solution)/shard_map/all_to_all | solution.py:68
  35.1 5.9 %reshape.541 = bf16[8192,2,8]{2,1,0:T(2,128)(2,1)} reshape(bf16[4,2,16384]{2,1,0:T(2,128)(2,1)S(1)} %all-to-all-done) | data formatting | bytes 524288
  41.0 8.9 %copy.68 = bf16[2,4,8,2048]{3,2,1,0:T(8,128)(2,1)S(1)} copy(bf16[2,4,8,2048]{2,0,3,1:T(2,128)(2,1)} %bitcast.376) | data formatting | bytes 524288 | tf_op jit(solution)/shard_map/all_to_all | solution.py:68
  49.9 3.3 %while.66 = (s32[]{:T(128)}, bf16[4,64,512]{2,1,0:T(8,128)(2,1)S(1)}, s32[4,512]{1,0:T(4,128)S(1)}, bf16[64,2048]{1,0:T(8,128)(2,1)S(1)}, s32[]{:T(128)}) while((s32[]{:T(128)}, bf16[4,64,512]{2,1,0:T(8,128)(2,1)S(1)}, s32[4,512]{1,0:T(4,128)S(1)}, bf16[64,2048]{1,0:T(8,128)(2,1)S(1)}, s32[]{:T(128)}) %tuple.141), condition=%wide.region_1.2_spmd.clone, body=%wide.region_0.1_spmd.clone.sunk | while | flops 135266304 | bytes 399429 | solution.py:26
  50.0 0.8 fusion.158
  50.8 0.8 fusion.158
  51.6 0.8 fusion.158
  52.4 0.8 fusion.158
  54.3 1.5 collective-permute-start
  55.8 4.6 %fusion.96 = (bf16[1,1,2048,128]{3,2,1,0:T(8,128)(2,1)}, bf16[1,1,2048,128]{3,2,1,0:T(8,128)(2,1)}, bf16[1,1,2048,128]{3,2,1,0:T(8,128)(2,1)S(1)}, bf16[1,1,2048...) fusion(bf16[6,2,2048,128]{3,2,1,0:T(8,128)(2,1)} %param.16), kind=kLoop, calls=%fused_computation.150 | loop fusion | bytes 12582912 | tf_op jit(solution)/shard_map/slice | solution.py:53
  60.4 0.9 reshape.471
  61.3 1.0 copy.70
  62.3 0.9 reshape.472
  63.2 1.0 copy.71
  64.8 1.1 fusion.97
  65.9 1.4 fusion.59
  67.5 1.6 fusion.58
  69.9 7.1 %while.67 = (s32[]{:T(128)}, bf16[4,64,512]{2,1,0:T(8,128)(2,1)S(1)}, s32[4,512]{1,0:T(4,128)S(1)}, bf16[64,2048]{1,0:T(8,128)(2,1)}, s32[]{:T(128)}) while((s32[]{:T(128)}, bf16[4,64,512]{2,1,0:T(8,128)(2,1)S(1)}, s32[4,512]{1,0:T(4,128)S(1)}, bf16[64,2048]{1,0:T(8,128)(2,1)}, s32[]{:T(128)}) %tuple.143), condition=%wide.region_3.4_spmd.clone, body=%wide.region_2.3_spmd.clone.sunk | while | flops 135266304 | bytes 399429 | solution.py:26
  70.0 1.7 fusion.160
  71.7 1.7 fusion.160
  73.5 1.7 fusion.160
  75.3 1.7 fusion.160
  77.1 0.9 copy.74
  78.0 1.1 convert_element_type.159
  79.8 2.7 %collective-permute-start.1 = (bf16[2,32,1,1024]{3,1,0,2:T(8,128)(2,1)}, bf16[2,32,1,1024]{3,1,0,2:T(8,128)(2,1)}, u32[]{:S(2)}, u32[]{:S(2)}) collective-permute-start(bf16[2,32,1,1024]{3,1,0,2:T(8,128)(2,1)} %get-tuple-element.308), channel_id=1, source_target_pairs={{0,8},{4,12},{8,0},{12,4},{16,24},{20,28},{24,16},{28,20},{32,40},... | collective-permute-start | bytes 393224 | tf_op jit(solution)/shard_map/ppermute | solution.py:11
  83.2 0.9 reshape.477
  84.1 1.0 copy.75
  85.1 1.4 collective-permute-done.1
  86.6 1.8 %reshape.478 = bf16[2,32,1,16,64]{4,3,1,0,2:T(8,128)(2,1)} reshape(bf16[2,32,1,1024]{3,1,0,2:T(8,128)(2,1)} %collective-permute-done.1) | data formatting | bytes 262144 | tf_op jit(solution)/shard_map/reshape | solution.py:46
  88.4 1.0 copy.76
  90.0 1.1 fusion.98
  91.6 1.4 fusion.56
  93.2 3.3 %while.68 = (s32[]{:T(128)}, bf16[4,64,512]{2,1,0:T(8,128)(2,1)S(1)}, s32[4,512]{1,0:T(4,128)S(1)}, bf16[64,2048]{1,0:T(8,128)(2,1)S(1)}, s32[]{:T(128)}) while((s32[]{:T(128)}, bf16[4,64,512]{2,1,0:T(8,128)(2,1)S(1)}, s32[4,512]{1,0:T(4,128)S(1)}, bf16[64,2048]{1,0:T(8,128)(2,1)S(1)}, s32[]{:T(128)}) %tuple.144), condition=%wide.region_5.6_spmd.clone, body=%wide.region_4.5_spmd.clone.sunk | while | flops 135266304 | bytes 399429 | solution.py:26
  93.3 0.8 fusion.162
  94.1 0.8 fusion.162
  94.9 0.8 fusion.162
  95.8 0.8 fusion.162
  98.3 3.9 %collective-permute-done.2 = bf16[2,32,1,1024]{3,1,0,2:T(8,128)(2,1)S(1)} collective-permute-done((bf16[2,32,1,1024]{3,1,0,2:T(8,128)(2,1)S(1)}, bf16[2,32,1,1024]{3,1,0,2:T(8,128)(2,1)S(1)}, u32[]{:S(2)}, u32[]{:S(2)}) %collective-permute-start.2) | collective-permute-done | bytes 131104 | tf_op jit(solution)/shard_map/ppermute | solution.py:11
  104.6 3.3 %while.69 = (s32[]{:T(128)}, bf16[4,64,512]{2,1,0:T(8,128)(2,1)S(1)}, s32[4,512]{1,0:T(4,128)S(1)}, bf16[64,2048]{1,0:T(8,128)(2,1)S(1)}, s32[]{:T(128)}) while((s32[]{:T(128)}, bf16[4,64,512]{2,1,0:T(8,128)(2,1)S(1)}, s32[4,512]{1,0:T(4,128)S(1)}, bf16[64,2048]{1,0:T(8,128)(2,1)S(1)}, s32[]{:T(128)}) %tuple.145), condition=%wide.region_7.8_spmd.clone, body=%wide.region_6.7_spmd.clone.sunk | while | flops 135266304 | bytes 399429 | solution.py:26
  104.6 0.8 fusion.164
  105.5 0.8 fusion.164
  107.1 0.8 fusion.164
  109.2 5.1 %collective-permute-done.3 = bf16[2,32,1,1024]{3,1,0,2:T(8,128)(2,1)S(1)} collective-permute-done((bf16[2,32,1,1024]{3,1,0,2:T(8,128)(2,1)S(1)}, bf16[2,32,1,1024]{3,1,0,2:T(8,128)(2,1)S(1)}, u32[]{:S(2)}, u32[]{:S(2)}) %collective-permute-start.3) | collective-permute-done | bytes 131104 | tf_op jit(solution)/shard_map/ppermute | solution.py:11
  116.7 3.3 %while.70 = (s32[]{:T(128)}, bf16[4,64,512]{2,1,0:T(8,128)(2,1)S(1)}, s32[4,512]{1,0:T(4,128)S(1)}, bf16[64,2048]{1,0:T(8,128)(2,1)S(1)}, s32[]{:T(128)}) while((s32[]{:T(128)}, bf16[4,64,512]{2,1,0:T(8,128)(2,1)S(1)}, s32[4,512]{1,0:T(4,128)S(1)}, bf16[64,2048]{1,0:T(8,128)(2,1)S(1)}, s32[]{:T(128)}) %tuple.146), condition=%wide.region_9.10_spmd.clone, body=%wide.region_8.9_spmd.clone.sunk | while | flops 135266304 | bytes 399429 | solution.py:26
  116.7 0.8 fusion.166
  117.5 0.8 fusion.166
  118.4 0.8 fusion.166
  120.4 1.7 collective-permute-start.4
  122.4 3.1 %collective-permute-done.4 = bf16[2,32,1,1024]{3,1,0,2:T(8,128)(2,1)S(1)} collective-permute-done((bf16[2,32,1,1024]{3,1,0,2:T(8,128)(2,1)S(1)}, bf16[2,32,1,1024]{3,1,0,2:T(8,128)(2,1)S(1)}, u32[]{:S(2)}, u32[]{:S(2)}) %collective-permute-start.4) | collective-permute-done | bytes 131104 | tf_op jit(solution)/shard_map/ppermute | solution.py:11
  127.8 3.3 %while.71 = (s32[]{:T(128)}, bf16[4,64,512]{2,1,0:T(8,128)(2,1)S(1)}, s32[4,512]{1,0:T(4,128)S(1)}, bf16[64,2048]{1,0:T(8,128)(2,1)S(1)}, s32[]{:T(128)}) while((s32[]{:T(128)}, bf16[4,64,512]{2,1,0:T(8,128)(2,1)S(1)}, s32[4,512]{1,0:T(4,128)S(1)}, bf16[64,2048]{1,0:T(8,128)(2,1)S(1)}, s32[]{:T(128)}) %tuple.142), condition=%wide.region_11.12_spmd.clone, body=%wide.region_10.11_spmd.clone.sunk | while | flops 135266304 | bytes 399429 | solution.py:26
  127.9 0.8 fusion.168
  128.7 0.8 fusion.168
  129.5 0.8 fusion.168
  130.4 0.8 fusion.168
  131.6 3.5 %collective-permute-start.5 = (bf16[2,32,1,1024]{3,1,0,2:T(8,128)(2,1)S(1)}, bf16[2,32,1,1024]{3,1,0,2:T(8,128)(2,1)S(1)}, u32[]{:S(2)}, u32[]{:S(2)}) collective-permute-start(bf16[2,32,1,1024]{3,1,0,2:T(8,128)(2,1)S(1)} %get-tuple-element.300), channel_id=1, source_target_pairs={{0,128},{4,132},{8,136},{12,140},{16,144},{20,148},{24,152},{28,15... | collective-permute-start | bytes 393224 | tf_op jit(solution)/shard_map/ppermute | solution.py:11
  135.4 3.0 %collective-permute-done.5 = bf16[2,32,1,1024]{3,1,0,2:T(8,128)(2,1)S(1)} collective-permute-done((bf16[2,32,1,1024]{3,1,0,2:T(8,128)(2,1)S(1)}, bf16[2,32,1,1024]{3,1,0,2:T(8,128)(2,1)S(1)}, u32[]{:S(2)}, u32[]{:S(2)}) %collective-permute-start.5) | collective-permute-done | bytes 131104 | tf_op jit(solution)/shard_map/ppermute | solution.py:11
  142.0 1.0 reshape.542
  143.0 19.4 %all_to_all.38 = bf16[64,2,1024]{2,1,0:T(2,128)(2,1)S(1)} all-to-all(bf16[64,2,1024]{2,1,0:T(2,128)(2,1)S(1)} %reshape.542), channel_id=1, replica_groups=mesh['pts'=64,'prb'=4] {'pts'}, dimensions={0} | all-to-all | bytes 524288 | tf_op jit(solution)/shard_map/all_to_all | solution.py:77
  162.9 1.3 copy.100
  164.6 15.1 %all_to_all.39 = bf16[4,2,16384]{2,1,0:T(2,128)(2,1)S(1)} all-to-all(bf16[4,2,16384]{2,1,0:T(2,128)(2,1)S(1)} %reshape.544), channel_id=1, replica_groups=mesh['pts'=64,'prb'=4] {'prb'}, dimensions={0} | all-to-all | bytes 524288 | tf_op jit(solution)/shard_map/all_to_all | solution.py:76
  180.5 1.2 reshape.507
  (152 shorter events, 23.9 us)
Async XLA Ops:
  0.0 22.3 %copy-start.7 = (s32[6,2048]{1,0:T(8,128)S(1)}, s32[6,2048]{1,0:T(8,128)}, u32[]{:S(2)}) copy-start(s32[6,2048]{1,0:T(8,128)} %param.17) | copy-start | bytes 147460
  14.8 20.3 %all-to-all-start = ((bf16[4,2,16384]{2,1,0:T(2,128)(2,1)}), bf16[4,2,16384]{2,1,0:T(2,128)(2,1)S(1)}, u32[]{:S(2)}, u32[]{:S(2)}) async-start(bf16[4,2,16384]{2,1,0:T(2,128)(2,1)} %reshape.540), calls=%async_computation | async-start | bytes 524288 | tf_op jit(solution)/shard_map/all_to_all | solution.py:68
  54.3 8.0 %collective-permute-start = (bf16[2,32,1,1024]{3,1,0,2:T(8,128)(2,1)}, bf16[2,32,1,1024]{3,1,0,2:T(8,128)(2,1)S(1)}, u32[]{:S(2)}, u32[]{:S(2)}) collective-permute-start(bf16[2,32,1,1024]{3,1,0,2:T(8,128)(2,1)} %get-tuple-element.310), channel_id=1, source_target_pairs={{0,4},{4,0},{8,12},{12,8},{16,20},{20,16},{24,28},{28,24},{32,36},... | collective-permute-start | bytes 393224 | tf_op jit(solution)/shard_map/ppermute | solution.py:11
  64.2 1.7 copy-start.5
  77.1 14.0 %copy-start.4 = (bf16[1,1,2048,128]{3,2,1,0:T(8,128)(2,1)S(1)}, bf16[1,1,2048,128]{3,2,1,0:T(8,128)(2,1)}, u32[]{:S(2)}) copy-start(bf16[1,1,2048,128]{3,2,1,0:T(8,128)(2,1)} %get-tuple-element.294) | copy-start | bytes 1572868
  79.8 6.8 %collective-permute-start.1 = (bf16[2,32,1,1024]{3,1,0,2:T(8,128)(2,1)}, bf16[2,32,1,1024]{3,1,0,2:T(8,128)(2,1)}, u32[]{:S(2)}, u32[]{:S(2)}) collective-permute-start(bf16[2,32,1,1024]{3,1,0,2:T(8,128)(2,1)} %get-tuple-element.308), channel_id=1, source_target_pairs={{0,8},{4,12},{8,0},{12,4},{16,24},{20,28},{24,16},{28,20},{32,40},... | collective-permute-start | bytes 393224 | tf_op jit(solution)/shard_map/ppermute | solution.py:11
  89.4 1.7 copy-start.6
  96.6 6.9 %copy-start.3 = (bf16[1,1,2048,128]{3,2,1,0:T(8,128)(2,1)S(1)}, bf16[1,1,2048,128]{3,2,1,0:T(8,128)(2,1)}, u32[]{:S(2)}) copy-start(bf16[1,1,2048,128]{3,2,1,0:T(8,128)(2,1)} %get-tuple-element.292) | copy-start | bytes 1572868
  97.0 5.2 %collective-permute-start.2 = (bf16[2,32,1,1024]{3,1,0,2:T(8,128)(2,1)S(1)}, bf16[2,32,1,1024]{3,1,0,2:T(8,128)(2,1)S(1)}, u32[]{:S(2)}, u32[]{:S(2)}) collective-permute-start(bf16[2,32,1,1024]{3,1,0,2:T(8,128)(2,1)S(1)} %get-tuple-element.306), channel_id=1, source_target_pairs={{0,16},{4,20},{8,24},{12,28},{16,0},{20,4},{24,8},{28,12},{32,48},... | collective-permute-start | bytes 393224 | tf_op jit(solution)/shard_map/ppermute | solution.py:11
  104.6 4.3 %copy-start.8 = (s32[2048]{0:T(1024)S(1)}, s32[2048]{0:T(1024)}, u32[]{:S(2)}) copy-start(s32[2048]{0:T(1024)} %get-tuple-element.236) | copy-start | bytes 24580
  107.9 7.6 %copy-start.2 = (bf16[1,1,2048,128]{3,2,1,0:T(8,128)(2,1)S(1)}, bf16[1,1,2048,128]{3,2,1,0:T(8,128)(2,1)}, u32[]{:S(2)}) copy-start(bf16[1,1,2048,128]{3,2,1,0:T(8,128)(2,1)} %get-tuple-element.290) | copy-start | bytes 1572868
  108.4 6.0 %collective-permute-start.3 = (bf16[2,32,1,1024]{3,1,0,2:T(8,128)(2,1)S(1)}, bf16[2,32,1,1024]{3,1,0,2:T(8,128)(2,1)S(1)}, u32[]{:S(2)}, u32[]{:S(2)}) collective-permute-start(bf16[2,32,1,1024]{3,1,0,2:T(8,128)(2,1)S(1)} %get-tuple-element.304), channel_id=1, source_target_pairs={{0,32},{4,36},{8,40},{12,44},{16,48},{20,52},{24,56},{28,60},{32,0... | collective-permute-start | bytes 393224 | tf_op jit(solution)/shard_map/ppermute | solution.py:11
  120.0 6.7 %copy-start.1 = (bf16[1,1,2048,128]{3,2,1,0:T(8,128)(2,1)S(1)}, bf16[1,1,2048,128]{3,2,1,0:T(8,128)(2,1)}, u32[]{:S(2)}) copy-start(bf16[1,1,2048,128]{3,2,1,0:T(8,128)(2,1)} %get-tuple-element.288) | copy-start | bytes 1572868
  120.4 5.1 %collective-permute-start.4 = (bf16[2,32,1,1024]{3,1,0,2:T(8,128)(2,1)S(1)}, bf16[2,32,1,1024]{3,1,0,2:T(8,128)(2,1)S(1)}, u32[]{:S(2)}, u32[]{:S(2)}) collective-permute-start(bf16[2,32,1,1024]{3,1,0,2:T(8,128)(2,1)S(1)} %get-tuple-element.302), channel_id=1, source_target_pairs={{0,64},{4,68},{8,72},{12,76},{16,80},{20,84},{24,88},{28,92},{32,9... | collective-permute-start | bytes 393224 | tf_op jit(solution)/shard_map/ppermute | solution.py:11
  131.2 8.4 %copy-start = (bf16[1,1,2048,128]{3,2,1,0:T(8,128)(2,1)S(1)}, bf16[1,1,2048,128]{3,2,1,0:T(8,128)(2,1)}, u32[]{:S(2)}) copy-start(bf16[1,1,2048,128]{3,2,1,0:T(8,128)(2,1)} %get-tuple-element.287) | copy-start | bytes 1572868
  131.6 6.8 %collective-permute-start.5 = (bf16[2,32,1,1024]{3,1,0,2:T(8,128)(2,1)S(1)}, bf16[2,32,1,1024]{3,1,0,2:T(8,128)(2,1)S(1)}, u32[]{:S(2)}, u32[]{:S(2)}) collective-permute-start(bf16[2,32,1,1024]{3,1,0,2:T(8,128)(2,1)S(1)} %get-tuple-element.300), channel_id=1, source_target_pairs={{0,128},{4,132},{8,136},{12,140},{16,144},{20,148},{24,152},{28,15... | collective-permute-start | bytes 393224 | tf_op jit(solution)/shard_map/ppermute | solution.py:11
where the time goes:
time: 184 us; the launch traced here: 182 us
  local copies, waits for them, and re-layouts  60.3 us (33%)
  matrix products  37.2 us (20%)
  blocking collectives  34.6 us (19%)
  waiting for transfers between devices  28.7 us (16%)
  starting transfers between devices  17.8 us (10%)
    unnamed x25, local copies, waits for them, and re-layouts  23 us
    dot_general x24, matrix products, one_block(): return jnp.dot(flat, selector, preferred_element_type=jnp.float32)  22.8 us
    all_to_all x1, blocking collectives, local(): lax.all_to_all(outgoing, 'pts', split_axis=3, concat_axis=3, tiled=True)  19.4 us
    ppermute x6, waiting for transfers between devices, from_partner(): lax.ppermute(value, axis, [(i, i ^ 1 << apart) for i in range(lax.axis_si...  16.7 us
    all_to_all x1, blocking collectives, local(): lax.all_to_all(lax.all_to_all(outgoing, 'pts', split_axis=3, concat_axis=...  15.1 us
    all_to_all x1, waiting for transfers between devices, local(): lax.all_to_all(probe_vectors, 'prb', split_axis=2, concat_axis=1, tiled=T...  12.1 us
    ppermute x6, starting transfers between devices, from_partner(): lax.ppermute(value, axis, [(i, i ^ 1 << apart) for i in range(lax.axis_si...  10.2 us
    all_to_all x1, local copies, waits for them, and re-layouts, local(): lax.all_to_all(probe_vectors, 'prb', split_axis=2, concat_axis=1, tiled=T...  8.88 us
  transfers between devices with their start and end apart: 7, of which 6 were waited for; matrix products, arithmetic and copies ran while one was open for 6% of the time, Pallas kernels for 0%

commit v1 on v0

v1 whole, which is shorter than its diff:
```python
import functools

import jax
import jax.numpy as jnp
from jax import lax
from jax.experimental import pallas as pl
from jax.experimental.pallas import tpu as pltpu
from jax.sharding import Mesh
from jax.sharding import PartitionSpec as P

RANK = 64
BLOCK = 2 * RANK
LEVELS = 6
LANES = 128
TILE = 16
BF16 = jnp.bfloat16
F32 = jnp.float32

ALONG_LANES = lax.GatherDimensionNumbers(
    offset_dims=(),
    collapsed_slice_dims=(1,),
    start_index_map=(1,),
    operand_batching_dims=(0,),
    start_indices_batching_dims=(0,),
)
BY_LAST = (((1,), (1,)), ((), ()))


def take_lanes(value, lanes):
    return lax.gather(
        value, lanes[..., None], ALONG_LANES, (1, 1), mode=lax.GatherScatterMode.PROMISE_IN_BOUNDS
    )


def gather_half(sources, order_ref, level, start, targets):
    half = order_ref.shape[1] // 2
    for t in range(half // LANES):
        columns = pl.ds(pl.multiple_of(start + t * LANES, LANES), LANES)
        index = jnp.broadcast_to(order_ref[level : level + 1, columns], (TILE, LANES))
        lane = (index % LANES).astype(jnp.int16)
        which = (index // LANES).astype(jnp.int16)
        picked = [None] * len(sources)
        for s in range(2 * half // LANES):
            here = which == jnp.int16(s)
            for g, source in enumerate(sources):
                value = take_lanes(source(s), lane)
                picked[g] = value if s == 0 else jnp.where(here, value, picked[g])
        for g, (ref, row) in enumerate(targets):
            ref[row : row + TILE, t * LANES : (t + 1) * LANES] = picked[g]


def turned(tile):
    wide = tile.astype(F32)
    return jnp.concatenate([-wide[8:], wide[:8]], 0).astype(BF16)


def joined_blocks(kept, got):
    pairs = [(k, g, turned(k), turned(g)) for k, g in zip(kept, got)]
    for m in range(kept[0].shape[1] // LANES):
        for side in range(2):
            at = slice(m * LANES + side * RANK, m * LANES + (side + 1) * RANK)
            yield 2 * m + side, [
                jnp.concatenate([k[:, at], g[:, at], tk[:, at], tg[:, at]], 1)
                for k, g, tk, tg in pairs
            ]


def block_factors(f_refs, k):
    return jnp.concatenate([ref[k * BLOCK : (k + 1) * BLOCK, :] for ref in f_refs], 1)


def upper_half(bit):
    return lax.axis_index("pts") // (1 << bit) % 2


def fetch_kernel(f_hbm, *refs):
    outs, sems = refs[:-1], refs[-1]
    copies = [
        pltpu.make_async_copy(f_hbm.at[i // 2, i % 2], out, sems.at[i]) for i, out in enumerate(outs)
    ]
    for copy in copies:
        copy.start()
    for copy in copies:
        copy.wait()


def start_kernel(x_ref, order_ref, *outs):
    upper = upper_half(0)
    zhi, core = lax.axis_index("h"), lax.axis_index("c")
    rows = order_ref.shape[1]
    half = rows // 2

    def columns(qh, qc):
        def column(s):
            at = pl.multiple_of((qh * 2 + qc) * rows + s * LANES, LANES)
            return jnp.concatenate(
                [x_ref[0, :, pl.ds(at, LANES)].astype(F32), x_ref[1, :, pl.ds(at, LANES)].astype(F32)], 0
            ).astype(BF16)

        return [column(s) for s in range(rows // LANES)]

    groups = [
        columns(zhi, core), columns(1 - zhi, core), columns(zhi, 1 - core), columns(1 - zhi, 1 - core),
    ]
    sources = [lambda s, g=g: g[s] for g in groups]
    gather_half(sources, order_ref, 0, upper * half, [(out, 0) for out in outs])
    gather_half(sources, order_ref, 0, (1 - upper) * half, [(out, TILE) for out in outs])


def tiles_of(refs, rows):
    if len(refs) == 4:
        tiles = [ref[row : row + TILE, :] for ref, row in zip(refs, rows)]
    else:
        tiles = [ref[row : row + TILE, :] for ref in refs for row in (0, TILE)]
    return tiles[:2], tiles[2:]


def gather_sent_kernel(core_ref, ref, sent_out):
    sent_out[:TILE, :] = core_ref[TILE:, :]
    sent_out[TILE:, :] = ref[TILE:, :]


def level_kernel(level, at, *refs):
    operands, (*f_refs, order_ref, sent_out, current) = refs[:-5], refs[-5:]
    kept, got = tiles_of(operands, at)
    for k, lhs in joined_blocks(kept, got):
        out = lax.dot_general(
            jnp.concatenate(lhs, 0), block_factors(f_refs, k), BY_LAST, preferred_element_type=F32
        )
        current[:, k * BLOCK : (k + 1) * BLOCK] = out.astype(BF16)
    half = order_ref.shape[1] // 2
    upper = upper_half(level + 1)
    count = len(kept)
    sources = [
        (lambda s, g=g: current[g * TILE : (g + 1) * TILE, s * LANES : (s + 1) * LANES])
        for g in range(count)
    ]
    gather_half(sources, order_ref, level + 1, (1 - upper) * half, [(sent_out, g * TILE) for g in range(count)])


def kept_kernel(level, current, order_ref, kept_out):
    half = order_ref.shape[1] // 2
    sources = [
        (lambda s, g=g: current[g * TILE : (g + 1) * TILE, s * LANES : (s + 1) * LANES]) for g in range(2)
    ]
    gather_half(sources, order_ref, level, upper_half(level) * half, [(kept_out, 0), (kept_out, TILE)])


def last_kernel(swap, kept_ref, got_ref, *refs):
    f_refs, out_ref = refs[:2], refs[2]
    lane = lax.broadcasted_iota(jnp.int32, (8, LANES), 1) // 32
    for k, rhs in joined_blocks(*tiles_of((kept_ref, got_ref), ())):
        rhs = rhs[::-1] if swap else rhs
        out = lax.dot_general(
            block_factors(f_refs, k), jnp.concatenate(rhs * 4, 0), BY_LAST, preferred_element_type=F32
        )
        for e in range(4):
            piece = out[e * 32 : e * 32 + 8]
            for rg in range(1, 4):
                piece = jnp.where(lane == rg, out[e * 32 + rg * 8 : e * 32 + rg * 8 + 8], piece)
            out_ref[4 * k + e] = piece.astype(BF16)


def merge_kernel(same_ref, other_ref, out_ref):
    zhi = lax.axis_index("h")
    slot = lax.broadcasted_iota(jnp.int32, same_ref.shape[1:], 1) // TILE % 2
    for e in range(same_ref.shape[0]):
        same, other = same_ref[e].astype(F32), other_ref[e].astype(F32)
        out_ref[2 * e + zhi] = jnp.where(slot == 0, same, other).astype(BF16)
        out_ref[2 * e + 1 - zhi] = jnp.where(slot == 0, other, same).astype(BF16)


def finish_kernel(in_ref, out_ref, wide):
    count = in_ref.shape[0] // 16
    wide[...] = in_ref[...].astype(F32)
    swap = (lax.axis_index("h") + lax.axis_index("c")) % 2 * TILE
    row = lax.broadcasted_iota(jnp.int32, (LANES, LANES), 0)
    col = lax.broadcasted_iota(jnp.int32, (LANES, LANES), 1)
    flipped = jnp.where(row // TILE % 2 == 0, row + swap, row - swap)
    pick = (flipped == col).astype(BF16)
    left = lax.broadcasted_iota(jnp.int32, (TILE, LANES), 1) < count
    for r8 in range(8):
        by_qh = [wide[pl.ds(qh * 8 + r8, count, stride=16), :] for qh in range(2)]
        straight = jnp.concatenate(by_qh, 0).astype(BF16)
        crossed = jnp.concatenate(by_qh[::-1], 0).astype(BF16)
        straight = lax.dot_general(pick, straight, BY_LAST, preferred_element_type=F32)
        crossed = lax.dot_general(pick, crossed, BY_LAST, preferred_element_type=F32)
        for rg in range(4):
            a = straight[rg * 32 : rg * 32 + 16]
            b = crossed[rg * 32 + 16 : rg * 32 + 32]
            at = (rg * 8 + r8) * 2 * LANES
            for qh, value in enumerate((jnp.where(left, a, b), jnp.where(left, b, a))):
                value = value.astype(BF16)
                lanes = slice(at + qh * LANES, at + (qh + 1) * LANES)
                out_ref[0, :, lanes] = value[:8]
                out_ref[1, :, lanes] = value[8:]


VMEM = pl.BlockSpec(memory_space=pltpu.VMEM)
HBM = pl.BlockSpec(memory_space=pltpu.HBM)


def bf16(*shape):
    return jax.ShapeDtypeStruct(shape, BF16)


def run(name, kernel, operands, outs, scratch=(), space=VMEM, limit=16, flops=1):
    return pl.pallas_call(
        kernel,
        out_shape=outs,
        in_specs=[space] * len(operands),
        out_specs=jax.tree.map(lambda _: VMEM, outs),
        scratch_shapes=scratch,
        compiler_params=pltpu.CompilerParams(vmem_limit_bytes=limit << 20),
        cost_estimate=pl.CostEstimate(flops=flops, bytes_accessed=1, transcendentals=0),
        name=name,
    )(*operands)


def local(probe_vectors, factors, row_orders):
    rows = row_orders.shape[1]
    half = rows // 2
    pts = lax.axis_size("pts")

    def across(value, bit):
        return lax.ppermute(value, "pts", [(i, i ^ 1 << bit) for i in range(pts)])

    def over(value, names):
        count = 2 ** len(names)
        return lax.ppermute(value, names, [(i, count - 1 - i) for i in range(count)])

    near, far, core_near, core_far = run(
        "start", start_kernel, (probe_vectors, row_orders), [bf16(2 * TILE, half)] * 4
    )
    core_far = over(core_far, ("h", "c"))
    core_near = over(core_near, "c")
    near, far, core_near = lax.optimization_barrier((near, far, core_near))
    far = over(far, "h")
    near_got = across(run("near", gather_sent_kernel, (core_near, near), bf16(2 * TILE, half)), 0)
    core_far, factors = lax.optimization_barrier((core_far, factors))
    layers = run(
        "fetch", fetch_kernel, (factors,), [bf16(rows, BLOCK)] * (2 * LEVELS),
        [pltpu.SemaphoreType.DMA((2 * LEVELS,))], HBM, 44,
    )
    far_got = across(run("far", gather_sent_kernel, (core_far, far), bf16(2 * TILE, half)), 0)
    chains = [((core_near, core_far), (near_got, far_got)), ((near, far), (near_got, far_got))]
    for level in range(LEVELS - 1):
        for which in range(2):
            kept, got = chains[which]
            sent, whole = run(
                "level", functools.partial(level_kernel, level, (0, 0, which * TILE, which * TILE)),
                (*kept, *got, *layers[2 * level : 2 * level + 2], row_orders),
                [bf16(2 * TILE, half), bf16(2 * TILE, rows)],
            )
            kept = run(
                "kept", functools.partial(kept_kernel, level + 1), (whole, row_orders), bf16(2 * TILE, half),
                flops=1 << 29,
            )
            kept, waiting = lax.optimization_barrier((kept, chains[1 - which][1]))
            chains[1 - which] = (chains[1 - which][0], waiting)
            chains[which] = ((kept,), (across(sent, level + 1),))
    def last(which, kept, got):
        return run(
            "last", functools.partial(last_kernel, which == 0),
            (*kept, *got, *layers[2 * LEVELS - 2 :]), bf16(pts, 8, LANES),
        )

    other = last(0, *chains[0])
    kept, got = chains[1]
    other, got = lax.optimization_barrier((other, got))
    other = over(other, "c")
    same = last(1, kept, got)
    outgoing = run("merge", merge_kernel, (same, other), bf16(2 * pts, 8, LANES))
    arrived = lax.all_to_all(outgoing, ("pts", "h"), 0, 0, tiled=True)
    return run(
        "finish", finish_kernel, (arrived.reshape(16 * pts, LANES),),
        bf16(2, 8, rows * 4), [pltpu.VMEM((16 * pts, LANES), F32)],
    )


def solution(mesh):
    fine = Mesh(mesh.devices.reshape(mesh.shape["pts"], 2, 2), ("pts", "h", "c"))
    placed = (P(None, ("h", "c"), "pts"), P(None, None, ("pts", "h", "c"), None), P())
    return jax.shard_map(
        local, mesh=fine, in_specs=placed, out_specs=P(None, ("h", "c"), "pts"), check_vma=False
    )
```

time: 184 us -> 86.7 us (0.47); the launches traced: 182 us -> 86.5 us
  local copies, waits for them, and re-layouts: 60.3 us -> 1.79 us
  matrix products: 37.2 us -> 0 us
  Pallas kernels: 0 us -> 17.9 us
  waiting for transfers between devices: 28.7 us -> 16.8 us
  blocking collectives: 34.6 us -> 24.5 us
  starting transfers between devices: 17.8 us -> 25.4 us
    dot_general x48 -> x0, matrix products: 37.2 us -> none  [the longest x24 22.8 us: one_block(): return jnp.dot(flat, selector, preferred_element_type=jnp.float32)]
    unnamed x25 -> x6, local copies, waits for them, and re-layouts: 23 us -> 1.79 us
    pallas_call x0 -> x28, Pallas kernels: none -> 17.9 us  [run(): pl.pallas_call(kernel, out_shape=outs, in_specs=[space] * len(operands),...]
    ppermute x6 -> x16, starting transfers between devices: 10.2 us -> 25.4 us  [the longest x12 17.7 us: across(): return lax.ppermute(value, 'pts', [(i, i ^ 1 << bit) for i in range(pts)])]
    all_to_all x1 -> x0, waiting for transfers between devices: 12.1 us -> none  [local(): lax.all_to_all(probe_vectors, 'prb', split_axis=2, concat_axis=1, tiled=T...]
    reshape x25 -> x0, local copies, waits for them, and re-layouts: 11.7 us -> none  [the longest x12 5.74 us: butterfly_level(): got_rows.reshape(2, probes_here, groups, nblocks, RANK)]
    all_to_all x2 -> x0, local copies, waits for them, and re-layouts: 10.2 us -> none  [the longest x1 8.88 us: local(): lax.all_to_all(probe_vectors, 'prb', split_axis=2, concat_axis=1, tiled=T...]
    all_to_all x2 -> x1, blocking collectives: 34.6 us -> 24.5 us  [local(): arrived = lax.all_to_all(outgoing, ('pts', 'h'), 0, 0, tiled=True)]
  transfers between devices with their start and end apart: 7 -> 16, of which waited for: 6 -> 11; matrix products, arithmetic and copies ran while one was open for 6% -> 0% of each run, Pallas kernels for 0% -> 17%
where the time goes in v1:
time: 86.7 us; the launch traced here: 86.5 us
  starting transfers between devices  25.4 us (29%)
  blocking collectives  24.5 us (28%)
  Pallas kernels  17.9 us (21%)
  waiting for transfers between devices  16.8 us (19%)
  local copies, waits for them, and re-layouts  1.79 us (2%)
    all_to_all x1, blocking collectives, local(): arrived = lax.all_to_all(outgoing, ('pts', 'h'), 0, 0, tiled=True)  24.5 us
    pallas_call x28, Pallas kernels, run(): pl.pallas_call(kernel, out_shape=outs, in_specs=[space] * len(operands),...  17.9 us
    ppermute x12, starting transfers between devices, across(): return lax.ppermute(value, 'pts', [(i, i ^ 1 << bit) for i in range(pts)])  17.7 us
    ppermute x12, waiting for transfers between devices, across(): return lax.ppermute(value, 'pts', [(i, i ^ 1 << bit) for i in range(pts)])  8.96 us
    ppermute x4, waiting for transfers between devices, over(): lax.ppermute(value, names, [(i, count - 1 - i) for i in range(count)])  7.8 us
    ppermute x4, starting transfers between devices, over(): lax.ppermute(value, names, [(i, count - 1 - i) for i in range(count)])  7.62 us
    unnamed x6, local copies, waits for them, and re-layouts  1.79 us
  transfers between devices with their start and end apart: 16, of which 11 were waited for; matrix products, arithmetic and copies ran while one was open for 0% of the time, Pallas kernels for 17%

profile of v1, /device:TPU:32, one launch (start us, length us, event | category | flops | bytes accessed | tf_op | source)
XLA Modules:
  0.0 86.5 jit_solution(10654653417759699919)
XLA Ops:
  0.0 0.0 copy-start
  0.0 0.8 copy-done
  0.8 0.0 copy-start.2
  0.8 0.9 %copy-done.2 = bf16[2,8,8192]{2,1,0:T(8,128)(2,1)S(1)} copy-done((bf16[2,8,8192]{2,1,0:T(8,128)(2,1)S(1)}, bf16[2,8,8192]{2,1,0:T(8,128)(2,1)}, u32[]{:S(2)}) %copy-start.2) | copy-done | bytes 262168
  1.8 1.2 %start.1 = (bf16[32,1024]{1,0:T(8,128)(2,1)S(1)}, bf16[32,1024]{1,0:T(8,128)(2,1)S(1)}, bf16[32,1024]{1,0:T(8,128)(2,1)S(1)}, bf16[32,1024]{1,0:T(8,128)(2,1)S(1)}) custom-call(bf16[2,8,8192]{2,1,0:T(8,128)(2,1)S(1)} %copy-done.2, s32[6,2048]{1,0:T(8,128)S(1)} %copy-done), custom_call_target="tpu_custom_call" | custom-call | flops 1 | bytes 1 | tf_op jit(solution)/shard_map/start/pallas_call | solution.py:208
  3.0 0.1 collective-permute-start
  3.1 6.4 %collective-permute-start.2 = (bf16[32,1024]{1,0:T(8,128)(2,1)S(1)}, bf16[32,1024]{1,0:T(8,128)(2,1)S(1)}, u32[]{:S(2)}, u32[]{:S(2)}) collective-permute-start(bf16[32,1024]{1,0:T(8,128)(2,1)S(1)} %get-tuple-element.75), channel_id=1, source_target_pairs={{0,3},{1,2},{2,1},{3,0},{4,7},{5,6},{6,5},{7,4},{8,11},{9,10},{10,... | collective-permute-start | bytes 196616 | tf_op jit(solution)/shard_map/ppermute | solution.py:230
  9.5 0.0 collective-permute-done.core_ref.refs_0_
  9.5 1.1 %collective-permute-start.1 = (bf16[32,1024]{1,0:T(8,128)(2,1)S(1)}, bf16[32,1024]{1,0:T(8,128)(2,1)S(1)}, u32[]{:S(2)}, u32[]{:S(2)}) collective-permute-start(bf16[32,1024]{1,0:T(8,128)(2,1)S(1)} %get-tuple-element.73), channel_id=1, source_target_pairs={{0,2},{2,0},{1,3},{3,1},{4,6},{6,4},{5,7},{7,5},{8,10},{10,8},{9,1... | collective-permute-start | bytes 196616 | tf_op jit(solution)/shard_map/ppermute | solution.py:230
  10.7 1.5 %collective-permute-start.3 = (bf16[32,1024]{1,0:T(8,128)(2,1)S(1)}, bf16[32,1024]{1,0:T(8,128)(2,1)S(1)}, u32[]{:S(2)}, u32[]{:S(2)}) collective-permute-start(bf16[32,1024]{1,0:T(8,128)(2,1)S(1)} %near.1), channel_id=1, source_target_pairs={{0,4},{4,0},{8,12},{12,8},{16,20},{20,16},{24,28},{28,24},{32,36},... | collective-permute-start | bytes 196616 | tf_op jit(solution)/shard_map/ppermute | solution.py:226
  12.2 2.4 %collective-permute-done.2.core_ref.refs_1_ = bf16[32,1024]{1,0:T(8,128)(2,1)S(1)} collective-permute-done((bf16[32,1024]{1,0:T(8,128)(2,1)S(1)}, bf16[32,1024]{1,0:T(8,128)(2,1)S(1)}, u32[]{:S(2)}, u32[]{:S(2)}) %collective-permute-start.2) | collective-permute-done | bytes 65568 | tf_op jit(solution)/shard_map/ppermute | solution.py:230
  14.6 4.6 %collective-permute-done.1.ref.refs_1_ = bf16[32,1024]{1,0:T(8,128)(2,1)S(1)} collective-permute-done((bf16[32,1024]{1,0:T(8,128)(2,1)S(1)}, bf16[32,1024]{1,0:T(8,128)(2,1)S(1)}, u32[]{:S(2)}, u32[]{:S(2)}) %collective-permute-start.1) | collective-permute-done | bytes 65568 | tf_op jit(solution)/shard_map/ppermute | solution.py:230
  19.1 1.5 %collective-permute-start.4 = (bf16[32,1024]{1,0:T(8,128)(2,1)S(1)}, bf16[32,1024]{1,0:T(8,128)(2,1)S(1)}, u32[]{:S(2)}, u32[]{:S(2)}) collective-permute-start(bf16[32,1024]{1,0:T(8,128)(2,1)S(1)} %far.1), channel_id=1, source_target_pairs={{0,4},{4,0},{8,12},{12,8},{16,20},{20,16},{24,28},{28,24},{32,36},... | collective-permute-start | bytes 196616 | tf_op jit(solution)/shard_map/ppermute | solution.py:226
  20.6 2.9 %fetch.1 = (bf16[2048,128]{1,0:T(8,128)(2,1)S(1)}, bf16[2048,128]{1,0:T(8,128)(2,1)S(1)}, bf16[2048,128]{1,0:T(8,128)(2,1)S(1)}, bf16[2048,128]{1,0:T(8,128)(2,1...) custom-call(bf16[6,2,2048,128]{3,2,1,0:T(8,128)(2,1)} %f_hbm), custom_call_target="tpu_custom_call" | custom-call | flops 1 | bytes 1 | tf_op jit(solution)/shard_map/fetch/pallas_call | solution.py:208
  23.5 0.0 collective-permute-done.3.refs_2_
  23.5 0.0 collective-permute-done.4.refs_3_
  23.5 0.0 copy-done.1
  23.5 0.8 level.10
  24.3 3.0 %collective-permute-start.5 = (bf16[32,1024]{1,0:T(8,128)(2,1)S(1)}, bf16[32,1024]{1,0:T(8,128)(2,1)S(1)}, u32[]{:S(2)}, u32[]{:S(2)}) collective-permute-start(bf16[32,1024]{1,0:T(8,128)(2,1)S(1)} %get-tuple-element.84), channel_id=1, source_target_pairs={{0,8},{4,12},{8,0},{12,4},{16,24},{20,28},{24,16},{28,20},{32,40},... | collective-permute-start | bytes 196616 | tf_op jit(solution)/shard_map/ppermute | solution.py:226
  27.3 0.4 kept.10.refs_0_
  27.6 0.8 level.11
  28.4 0.7 collective-permute-start.6
  29.2 0.4 kept.11.refs_0_
  29.5 1.3 %collective-permute-done.5.refs_1_ = bf16[32,1024]{1,0:T(8,128)(2,1)S(1)} collective-permute-done((bf16[32,1024]{1,0:T(8,128)(2,1)S(1)}, bf16[32,1024]{1,0:T(8,128)(2,1)S(1)}, u32[]{:S(2)}, u32[]{:S(2)}) %collective-permute-start.5) | collective-permute-done | bytes 65568 | tf_op jit(solution)/shard_map/ppermute | solution.py:226
  30.8 0.8 level.12
  31.6 0.1 collective-permute-start.7
  31.7 0.4 kept.12.refs_0_
  32.1 2.2 %collective-permute-done.6.refs_1_ = bf16[32,1024]{1,0:T(8,128)(2,1)S(1)} collective-permute-done((bf16[32,1024]{1,0:T(8,128)(2,1)S(1)}, bf16[32,1024]{1,0:T(8,128)(2,1)S(1)}, u32[]{:S(2)}, u32[]{:S(2)}) %collective-permute-start.6) | collective-permute-done | bytes 65568 | tf_op jit(solution)/shard_map/ppermute | solution.py:226
  34.3 0.8 level.13
  35.1 0.4 collective-permute-start.8
  35.5 0.4 kept.13.refs_0_
  35.8 0.1 collective-permute-done.7.refs_1_
  36.0 0.8 level.14
  36.7 1.8 %collective-permute-start.9 = (bf16[32,1024]{1,0:T(8,128)(2,1)S(1)}, bf16[32,1024]{1,0:T(8,128)(2,1)S(1)}, u32[]{:S(2)}, u32[]{:S(2)}) collective-permute-start(bf16[32,1024]{1,0:T(8,128)(2,1)S(1)} %get-tuple-element.104), channel_id=1, source_target_pairs={{0,32},{4,36},{8,40},{12,44},{16,48},{20,52},{24,56},{28,60},{32,0... | collective-permute-start | bytes 196616 | tf_op jit(solution)/shard_map/ppermute | solution.py:226
  38.6 0.4 kept.14.refs_0_
  38.9 0.6 collective-permute-done.8.refs_1_
  39.5 0.8 level.15
  40.3 1.0 %collective-permute-start.10 = (bf16[32,1024]{1,0:T(8,128)(2,1)S(1)}, bf16[32,1024]{1,0:T(8,128)(2,1)S(1)}, u32[]{:S(2)}, u32[]{:S(2)}) collective-permute-start(bf16[32,1024]{1,0:T(8,128)(2,1)S(1)} %get-tuple-element.111), channel_id=1, source_target_pairs={{0,32},{4,36},{8,40},{12,44},{16,48},{20,52},{24,56},{28,60},{32,0... | collective-permute-start | bytes 196616 | tf_op jit(solution)/shard_map/ppermute | solution.py:226
  41.3 0.4 kept.15.refs_0_
  41.6 0.4 collective-permute-done.9.refs_1_
  42.1 0.8 level.16
  42.8 1.7 %collective-permute-start.11 = (bf16[32,1024]{1,0:T(8,128)(2,1)S(1)}, bf16[32,1024]{1,0:T(8,128)(2,1)S(1)}, u32[]{:S(2)}, u32[]{:S(2)}) collective-permute-start(bf16[32,1024]{1,0:T(8,128)(2,1)S(1)} %get-tuple-element.114), channel_id=1, source_target_pairs={{0,64},{4,68},{8,72},{12,76},{16,80},{20,84},{24,88},{28,92},{32,9... | collective-permute-start | bytes 196616 | tf_op jit(solution)/shard_map/ppermute | solution.py:226
  44.5 0.4 kept.16.refs_0_
  44.9 0.8 collective-permute-done.10.refs_1_
  45.7 0.8 level.17
  46.5 1.7 %collective-permute-start.12 = (bf16[32,1024]{1,0:T(8,128)(2,1)S(1)}, bf16[32,1024]{1,0:T(8,128)(2,1)S(1)}, u32[]{:S(2)}, u32[]{:S(2)}) collective-permute-start(bf16[32,1024]{1,0:T(8,128)(2,1)S(1)} %get-tuple-element.121), channel_id=1, source_target_pairs={{0,64},{4,68},{8,72},{12,76},{16,80},{20,84},{24,88},{28,92},{32,9... | collective-permute-start | bytes 196616 | tf_op jit(solution)/shard_map/ppermute | solution.py:226
  48.1 0.4 kept.17.refs_0_
  48.5 0.0 collective-permute-done.11.refs_1_
  48.5 0.8 level.18
  49.3 0.4 kept.18.kept_ref
  49.7 3.0 %collective-permute-start.13 = (bf16[32,1024]{1,0:T(8,128)(2,1)S(1)}, bf16[32,1024]{1,0:T(8,128)(2,1)S(1)}, u32[]{:S(2)}, u32[]{:S(2)}) collective-permute-start(bf16[32,1024]{1,0:T(8,128)(2,1)S(1)} %get-tuple-element.124), channel_id=1, source_target_pairs={{0,128},{4,132},{8,136},{12,140},{16,144},{20,148},{24,152},{28,15... | collective-permute-start | bytes 196616 | tf_op jit(solution)/shard_map/ppermute | solution.py:226
  52.7 0.0 collective-permute-done.12.refs_1_
  52.7 0.8 level.19
  53.4 1.4 %collective-permute-start.14 = (bf16[32,1024]{1,0:T(8,128)(2,1)S(1)}, bf16[32,1024]{1,0:T(8,128)(2,1)S(1)}, u32[]{:S(2)}, u32[]{:S(2)}) collective-permute-start(bf16[32,1024]{1,0:T(8,128)(2,1)S(1)} %get-tuple-element.130), channel_id=1, source_target_pairs={{0,128},{4,132},{8,136},{12,140},{16,144},{20,148},{24,152},{28,15... | collective-permute-start | bytes 196616 | tf_op jit(solution)/shard_map/ppermute | solution.py:226
  54.9 0.4 kept.19.kept_ref
  55.2 0.3 collective-permute-done.13.got_ref
  55.5 0.5 last.2
  56.0 3.3 %collective-permute-done.14.got_ref = bf16[32,1024]{1,0:T(8,128)(2,1)S(1)} collective-permute-done((bf16[32,1024]{1,0:T(8,128)(2,1)S(1)}, bf16[32,1024]{1,0:T(8,128)(2,1)S(1)}, u32[]{:S(2)}, u32[]{:S(2)}) %collective-permute-start.14) | collective-permute-done | bytes 65568 | tf_op jit(solution)/shard_map/ppermute | solution.py:226
  59.3 0.0 collective-permute-start.15
  59.3 0.5 last.3.same_ref
  59.8 0.8 collective-permute-done.15.other_ref
  60.7 0.1 merge.1
  60.7 24.5 %all_to_all.5 = bf16[128,8,128]{2,1,0:T(8,128)(2,1)S(1)} all-to-all(bf16[128,8,128]{2,1,0:T(8,128)(2,1)S(1)} %merge.1), channel_id=1, replica_groups=mesh['pts'=64,'h'=2,'c'=2] {'pts','h'}, dimensions={0} | all-to-all | bytes 524288 | tf_op jit(solution)/shard_map/all_to_all | solution.py:274
  85.3 1.2 %finish.1 = bf16[2,8,8192]{2,1,0:T(8,128)(2,1)} custom-call(bf16[1024,128]{1,0:T(8,128)(2,1)S(1)} %bitcast.1), custom_call_target="tpu_custom_call" | custom-call | flops 1 | bytes 1 | tf_op jit(solution)/shard_map/finish/pallas_call | solution.py:208
  (3 shorter events, 0.0 us)
Async XLA Ops:
  0.0 0.8 copy-start
  0.8 0.9 %copy-start.2 = (bf16[2,8,8192]{2,1,0:T(8,128)(2,1)S(1)}, bf16[2,8,8192]{2,1,0:T(8,128)(2,1)}, u32[]{:S(2)}) copy-start(bf16[2,8,8192]{2,1,0:T(8,128)(2,1)} %x_ref.1) | copy-start | bytes 786436
  1.8 21.7 %copy-start.1 = (s32[6,2048]{1,0:T(8,128)S(1)}, s32[6,2048]{1,0:T(8,128)}, u32[]{:S(2)}) copy-start(s32[6,2048]{1,0:T(8,128)} %order_ref.21) | copy-start | bytes 147460
  3.0 6.5 %collective-permute-start = (bf16[32,1024]{1,0:T(8,128)(2,1)S(1)}, bf16[32,1024]{1,0:T(8,128)(2,1)S(1)}, u32[]{:S(2)}, u32[]{:S(2)}) collective-permute-start(bf16[32,1024]{1,0:T(8,128)(2,1)S(1)} %get-tuple-element.71), channel_id=1, source_target_pairs={{0,1},{1,0},{2,3},{3,2},{4,5},{5,4},{6,7},{7,6},{8,9},{9,8},{10,11... | collective-permute-start | bytes 196616 | tf_op jit(solution)/shard_map/ppermute | solution.py:230
  3.1 11.4 %collective-permute-start.2 = (bf16[32,1024]{1,0:T(8,128)(2,1)S(1)}, bf16[32,1024]{1,0:T(8,128)(2,1)S(1)}, u32[]{:S(2)}, u32[]{:S(2)}) collective-permute-start(bf16[32,1024]{1,0:T(8,128)(2,1)S(1)} %get-tuple-element.75), channel_id=1, source_target_pairs={{0,3},{1,2},{2,1},{3,0},{4,7},{5,6},{6,5},{7,4},{8,11},{9,10},{10,... | collective-permute-start | bytes 196616 | tf_op jit(solution)/shard_map/ppermute | solution.py:230
  9.5 9.6 %collective-permute-start.1 = (bf16[32,1024]{1,0:T(8,128)(2,1)S(1)}, bf16[32,1024]{1,0:T(8,128)(2,1)S(1)}, u32[]{:S(2)}, u32[]{:S(2)}) collective-permute-start(bf16[32,1024]{1,0:T(8,128)(2,1)S(1)} %get-tuple-element.73), channel_id=1, source_target_pairs={{0,2},{2,0},{1,3},{3,1},{4,6},{6,4},{5,7},{7,5},{8,10},{10,8},{9,1... | collective-permute-start | bytes 196616 | tf_op jit(solution)/shard_map/ppermute | solution.py:230
  10.7 12.8 %collective-permute-start.3 = (bf16[32,1024]{1,0:T(8,128)(2,1)S(1)}, bf16[32,1024]{1,0:T(8,128)(2,1)S(1)}, u32[]{:S(2)}, u32[]{:S(2)}) collective-permute-start(bf16[32,1024]{1,0:T(8,128)(2,1)S(1)} %near.1), channel_id=1, source_target_pairs={{0,4},{4,0},{8,12},{12,8},{16,20},{20,16},{24,28},{28,24},{32,36},... | collective-permute-start | bytes 196616 | tf_op jit(solution)/shard_map/ppermute | solution.py:226
  19.1 4.4 %collective-permute-start.4 = (bf16[32,1024]{1,0:T(8,128)(2,1)S(1)}, bf16[32,1024]{1,0:T(8,128)(2,1)S(1)}, u32[]{:S(2)}, u32[]{:S(2)}) collective-permute-start(bf16[32,1024]{1,0:T(8,128)(2,1)S(1)} %far.1), channel_id=1, source_target_pairs={{0,4},{4,0},{8,12},{12,8},{16,20},{20,16},{24,28},{28,24},{32,36},... | collective-permute-start | bytes 196616 | tf_op jit(solution)/shard_map/ppermute | solution.py:226
  24.3 6.5 %collective-permute-start.5 = (bf16[32,1024]{1,0:T(8,128)(2,1)S(1)}, bf16[32,1024]{1,0:T(8,128)(2,1)S(1)}, u32[]{:S(2)}, u32[]{:S(2)}) collective-permute-start(bf16[32,1024]{1,0:T(8,128)(2,1)S(1)} %get-tuple-element.84), channel_id=1, source_target_pairs={{0,8},{4,12},{8,0},{12,4},{16,24},{20,28},{24,16},{28,20},{32,40},... | collective-permute-start | bytes 196616 | tf_op jit(solution)/shard_map/ppermute | solution.py:226
  28.4 5.9 %collective-permute-start.6 = (bf16[32,1024]{1,0:T(8,128)(2,1)S(1)}, bf16[32,1024]{1,0:T(8,128)(2,1)S(1)}, u32[]{:S(2)}, u32[]{:S(2)}) collective-permute-start(bf16[32,1024]{1,0:T(8,128)(2,1)S(1)} %get-tuple-element.91), channel_id=1, source_target_pairs={{0,8},{4,12},{8,0},{12,4},{16,24},{20,28},{24,16},{28,20},{32,40},... | collective-permute-start | bytes 196616 | tf_op jit(solution)/shard_map/ppermute | solution.py:226
  31.6 4.4 %collective-permute-start.7 = (bf16[32,1024]{1,0:T(8,128)(2,1)S(1)}, bf16[32,1024]{1,0:T(8,128)(2,1)S(1)}, u32[]{:S(2)}, u32[]{:S(2)}) collective-permute-start(bf16[32,1024]{1,0:T(8,128)(2,1)S(1)} %get-tuple-element.94), channel_id=1, source_target_pairs={{0,16},{4,20},{8,24},{12,28},{16,0},{20,4},{24,8},{28,12},{32,48},... | collective-permute-start | bytes 196616 | tf_op jit(solution)/shard_map/ppermute | solution.py:226
  35.1 4.4 %collective-permute-start.8 = (bf16[32,1024]{1,0:T(8,128)(2,1)S(1)}, bf16[32,1024]{1,0:T(8,128)(2,1)S(1)}, u32[]{:S(2)}, u32[]{:S(2)}) collective-permute-start(bf16[32,1024]{1,0:T(8,128)(2,1)S(1)} %get-tuple-element.101), channel_id=1, source_target_pairs={{0,16},{4,20},{8,24},{12,28},{16,0},{20,4},{24,8},{28,12},{32,48},... | collective-permute-start | bytes 196616 | tf_op jit(solution)/shard_map/ppermute | solution.py:226
  36.7 5.3 %collective-permute-start.9 = (bf16[32,1024]{1,0:T(8,128)(2,1)S(1)}, bf16[32,1024]{1,0:T(8,128)(2,1)S(1)}, u32[]{:S(2)}, u32[]{:S(2)}) collective-permute-start(bf16[32,1024]{1,0:T(8,128)(2,1)S(1)} %get-tuple-element.104), channel_id=1, source_target_pairs={{0,32},{4,36},{8,40},{12,44},{16,48},{20,52},{24,56},{28,60},{32,0... | collective-permute-start | bytes 196616 | tf_op jit(solution)/shard_map/ppermute | solution.py:226
  40.3 5.4 %collective-permute-start.10 = (bf16[32,1024]{1,0:T(8,128)(2,1)S(1)}, bf16[32,1024]{1,0:T(8,128)(2,1)S(1)}, u32[]{:S(2)}, u32[]{:S(2)}) collective-permute-start(bf16[32,1024]{1,0:T(8,128)(2,1)S(1)} %get-tuple-element.111), channel_id=1, source_target_pairs={{0,32},{4,36},{8,40},{12,44},{16,48},{20,52},{24,56},{28,60},{32,0... | collective-permute-start | bytes 196616 | tf_op jit(solution)/shard_map/ppermute | solution.py:226
  42.8 5.7 %collective-permute-start.11 = (bf16[32,1024]{1,0:T(8,128)(2,1)S(1)}, bf16[32,1024]{1,0:T(8,128)(2,1)S(1)}, u32[]{:S(2)}, u32[]{:S(2)}) collective-permute-start(bf16[32,1024]{1,0:T(8,128)(2,1)S(1)} %get-tuple-element.114), channel_id=1, source_target_pairs={{0,64},{4,68},{8,72},{12,76},{16,80},{20,84},{24,88},{28,92},{32,9... | collective-permute-start | bytes 196616 | tf_op jit(solution)/shard_map/ppermute | solution.py:226
  46.5 6.2 %collective-permute-start.12 = (bf16[32,1024]{1,0:T(8,128)(2,1)S(1)}, bf16[32,1024]{1,0:T(8,128)(2,1)S(1)}, u32[]{:S(2)}, u32[]{:S(2)}) collective-permute-start(bf16[32,1024]{1,0:T(8,128)(2,1)S(1)} %get-tuple-element.121), channel_id=1, source_target_pairs={{0,64},{4,68},{8,72},{12,76},{16,80},{20,84},{24,88},{28,92},{32,9... | collective-permute-start | bytes 196616 | tf_op jit(solution)/shard_map/ppermute | solution.py:226
  49.7 5.9 %collective-permute-start.13 = (bf16[32,1024]{1,0:T(8,128)(2,1)S(1)}, bf16[32,1024]{1,0:T(8,128)(2,1)S(1)}, u32[]{:S(2)}, u32[]{:S(2)}) collective-permute-start(bf16[32,1024]{1,0:T(8,128)(2,1)S(1)} %get-tuple-element.124), channel_id=1, source_target_pairs={{0,128},{4,132},{8,136},{12,140},{16,144},{20,148},{24,152},{28,15... | collective-permute-start | bytes 196616 | tf_op jit(solution)/shard_map/ppermute | solution.py:226
  53.4 5.9 %collective-permute-start.14 = (bf16[32,1024]{1,0:T(8,128)(2,1)S(1)}, bf16[32,1024]{1,0:T(8,128)(2,1)S(1)}, u32[]{:S(2)}, u32[]{:S(2)}) collective-permute-start(bf16[32,1024]{1,0:T(8,128)(2,1)S(1)} %get-tuple-element.130), channel_id=1, source_target_pairs={{0,128},{4,132},{8,136},{12,140},{16,144},{20,148},{24,152},{28,15... | collective-permute-start | bytes 196616 | tf_op jit(solution)/shard_map/ppermute | solution.py:226
  59.3 1.3 %collective-permute-start.15 = (bf16[64,8,128]{2,1,0:T(8,128)(2,1)S(1)}, bf16[64,8,128]{2,1,0:T(8,128)(2,1)S(1)}, u32[]{:S(2)}, u32[]{:S(2)}) collective-permute-start(bf16[64,8,128]{2,1,0:T(8,128)(2,1)S(1)} %last.2), channel_id=1, source_target_pairs={{0,1},{1,0},{2,3},{3,2},{4,5},{5,4},{6,7},{7,6},{8,9},{9,8},{10,11... | collective-permute-start | bytes 393224 | tf_op jit(solution)/shard_map/ppermute | solution.py:230

commit v2 on v1

--- a/solution.py
+++ b/solution.py
@@ -113,6 +113,10 @@
     else:
         tiles = [ref[row : row + TILE, :] for ref in refs for row in (0, TILE)]
     return tiles[:2], tiles[2:]
+
+
+def sent_kernel(ref, sent_out):
+    sent_out[...] = ref[TILE:, :]
 
 
 def gather_sent_kernel(core_ref, ref, sent_out):
@@ -242,13 +246,16 @@
         "fetch", fetch_kernel, (factors,), [bf16(rows, BLOCK)] * (2 * LEVELS),
         [pltpu.SemaphoreType.DMA((2 * LEVELS,))], HBM, 44,
     )
-    far_got = across(run("far", gather_sent_kernel, (core_far, far), bf16(2 * TILE, half)), 0)
-    chains = [((core_near, core_far), (near_got, far_got)), ((near, far), (near_got, far_got))]
+    core_got = across(run("core_sent", sent_kernel, (core_far,), bf16(TILE, half)), 0)
+    far_sent = run("far_sent", sent_kernel, (far,), bf16(TILE, half))
+    core_kept, far_sent = lax.optimization_barrier((core_near, far_sent))
+    far_got = across(far_sent, 0)
+    chains = [((core_kept, core_far), (near_got, core_got)), ((near, far), (near_got, far_got))]
     for level in range(LEVELS - 1):
         for which in range(2):
             kept, got = chains[which]
             sent, whole = run(
-                "level", functools.partial(level_kernel, level, (0, 0, which * TILE, which * TILE)),
+                "level", functools.partial(level_kernel, level, (0, 0, which * TILE, 0)),
                 (*kept, *got, *layers[2 * level : 2 * level + 2], row_orders),
                 [bf16(2 * TILE, half), bf16(2 * TILE, rows)],
             )

time: 86.7 us -> 83.6 us (0.964)
  waiting for transfers between devices: 16.8 us -> 11.7 us
  starting transfers between devices: 25.4 us -> 27.5 us
    ppermute x4, waiting for transfers between devices: 7.8 us -> 3.41 us  [over(): lax.ppermute(value, names, [(i, count - 1 - i) for i in range(count)])]
    ppermute x12 -> x13, starting transfers between devices: 17.7 us -> 19.8 us  [across(): return lax.ppermute(value, 'pts', [(i, i ^ 1 << bit) for i in range(pts)])]
    ppermute x12 -> x13, waiting for transfers between devices: 8.96 us -> 8.25 us  [across(): return lax.ppermute(value, 'pts', [(i, i ^ 1 << bit) for i in range(pts)])]
    pallas_call x28 -> x29, Pallas kernels: 17.9 us -> 17.9 us  [run(): pl.pallas_call(kernel, out_shape=outs, in_specs=[space] * len(operands),...]
  transfers between devices with their start and end apart: 16 -> 17, of which waited for: 11 -> 11; matrix products, arithmetic and copies ran while one was open for 0% -> 0% of each run, Pallas kernels for 17% -> 18%
where the time goes in v2:
time: 83.6 us; the launch traced here: 83.4 us
  starting transfers between devices  27.5 us (33%)
  blocking collectives  24.5 us (29%)
  Pallas kernels  17.9 us (21%)
  waiting for transfers between devices  11.7 us (14%)
  local copies, waits for them, and re-layouts  1.79 us (2%)
    all_to_all x1, blocking collectives, local(): arrived = lax.all_to_all(outgoing, ('pts', 'h'), 0, 0, tiled=True)  24.5 us
    ppermute x13, starting transfers between devices, across(): return lax.ppermute(value, 'pts', [(i, i ^ 1 << bit) for i in range(pts)])  19.8 us
    pallas_call x29, Pallas kernels, run(): pl.pallas_call(kernel, out_shape=outs, in_specs=[space] * len(operands),...  17.9 us
    ppermute x13, waiting for transfers between devices, across(): return lax.ppermute(value, 'pts', [(i, i ^ 1 << bit) for i in range(pts)])  8.25 us
    ppermute x4, starting transfers between devices, over(): lax.ppermute(value, names, [(i, count - 1 - i) for i in range(count)])  7.62 us
    ppermute x4, waiting for transfers between devices, over(): lax.ppermute(value, names, [(i, count - 1 - i) for i in range(count)])  3.41 us
    unnamed x6, local copies, waits for them, and re-layouts  1.79 us
  transfers between devices with their start and end apart: 17, of which 11 were waited for; matrix products, arithmetic and copies ran while one was open for 0% of the time, Pallas kernels for 18%

profile of v2, /device:TPU:32, one launch (start us, length us, event | category | flops | bytes accessed | tf_op | source)
XLA Modules:
  0.0 83.4 jit_solution(9109125823981220874)
XLA Ops:
  0.0 0.8 %copy-done = s32[6,2048]{1,0:T(8,128)S(1)} copy-done((s32[6,2048]{1,0:T(8,128)S(1)}, s32[6,2048]{1,0:T(8,128)}, u32[]{:S(2)}) %copy-start) | copy-done | bytes 49176
  0.8 0.9 %copy-done.2 = bf16[2,8,8192]{2,1,0:T(8,128)(2,1)S(1)} copy-done((bf16[2,8,8192]{2,1,0:T(8,128)(2,1)S(1)}, bf16[2,8,8192]{2,1,0:T(8,128)(2,1)}, u32[]{:S(2)}) %copy-start.2) | copy-done | bytes 262168
  1.8 1.2 %start.1 = (bf16[32,1024]{1,0:T(8,128)(2,1)S(1)}, bf16[32,1024]{1,0:T(8,128)(2,1)S(1)}, bf16[32,1024]{1,0:T(8,128)(2,1)S(1)}, bf16[32,1024]{1,0:T(8,128)(2,1)S(1)}) custom-call(bf16[2,8,8192]{2,1,0:T(8,128)(2,1)S(1)} %copy-done.2, s32[6,2048]{1,0:T(8,128)S(1)} %copy-done), custom_call_target="tpu_custom_call" | custom-call | flops 1 | bytes 1 | tf_op jit(solution)/shard_map/start/pallas_call | solution.py:212
  3.0 0.1 collective-permute-start
  3.1 6.4 %collective-permute-start.2 = (bf16[32,1024]{1,0:T(8,128)(2,1)S(1)}, bf16[32,1024]{1,0:T(8,128)(2,1)S(1)}, u32[]{:S(2)}, u32[]{:S(2)}) collective-permute-start(bf16[32,1024]{1,0:T(8,128)(2,1)S(1)} %get-tuple-element.78), channel_id=1, source_target_pairs={{0,3},{1,2},{2,1},{3,0},{4,7},{5,6},{6,5},{7,4},{8,11},{9,10},{10,... | collective-permute-start | bytes 196616 | tf_op jit(solution)/shard_map/ppermute | solution.py:234
  9.5 0.0 collective-permute-done.core_ref.refs_0_
  9.5 1.1 %collective-permute-start.1 = (bf16[32,1024]{1,0:T(8,128)(2,1)S(1)}, bf16[32,1024]{1,0:T(8,128)(2,1)S(1)}, u32[]{:S(2)}, u32[]{:S(2)}) collective-permute-start(bf16[32,1024]{1,0:T(8,128)(2,1)S(1)} %get-tuple-element.75), channel_id=1, source_target_pairs={{0,2},{2,0},{1,3},{3,1},{4,6},{6,4},{5,7},{7,5},{8,10},{10,8},{9,1... | collective-permute-start | bytes 196616 | tf_op jit(solution)/shard_map/ppermute | solution.py:234
  10.7 1.5 %collective-permute-start.3 = (bf16[32,1024]{1,0:T(8,128)(2,1)S(1)}, bf16[32,1024]{1,0:T(8,128)(2,1)S(1)}, u32[]{:S(2)}, u32[]{:S(2)}) collective-permute-start(bf16[32,1024]{1,0:T(8,128)(2,1)S(1)} %near.1), channel_id=1, source_target_pairs={{0,4},{4,0},{8,12},{12,8},{16,20},{20,16},{24,28},{28,24},{32,36},... | collective-permute-start | bytes 196616 | tf_op jit(solution)/shard_map/ppermute | solution.py:230
  12.2 2.4 %collective-permute-done.2.ref.refs_1_ = bf16[32,1024]{1,0:T(8,128)(2,1)S(1)} collective-permute-done((bf16[32,1024]{1,0:T(8,128)(2,1)S(1)}, bf16[32,1024]{1,0:T(8,128)(2,1)S(1)}, u32[]{:S(2)}, u32[]{:S(2)}) %collective-permute-start.2) | collective-permute-done | bytes 65568 | tf_op jit(solution)/shard_map/ppermute | solution.py:234
  14.6 1.5 %collective-permute-start.4 = (bf16[16,1024]{1,0:T(8,128)(2,1)S(1)}, bf16[16,1024]{1,0:T(8,128)(2,1)S(1)}, u32[]{:S(2)}, u32[]{:S(2)}) collective-permute-start(bf16[16,1024]{1,0:T(8,128)(2,1)S(1)} %core_sent.1), channel_id=1, source_target_pairs={{0,4},{4,0},{8,12},{12,8},{16,20},{20,16},{24,28},{28,24},{32,36},... | collective-permute-start | bytes 98312 | tf_op jit(solution)/shard_map/ppermute | solution.py:230
  16.1 2.9 %fetch.1 = (bf16[2048,128]{1,0:T(8,128)(2,1)S(1)}, bf16[2048,128]{1,0:T(8,128)(2,1)S(1)}, bf16[2048,128]{1,0:T(8,128)(2,1)S(1)}, bf16[2048,128]{1,0:T(8,128)(2,1...) custom-call(bf16[6,2,2048,128]{3,2,1,0:T(8,128)(2,1)} %f_hbm), custom_call_target="tpu_custom_call" | custom-call | flops 1 | bytes 1 | tf_op jit(solution)/shard_map/fetch/pallas_call | solution.py:212
  18.9 0.2 collective-permute-done.1.ref.refs_1_
  19.1 1.5 %collective-permute-start.5 = (bf16[16,1024]{1,0:T(8,128)(2,1)S(1)}, bf16[16,1024]{1,0:T(8,128)(2,1)S(1)}, u32[]{:S(2)}, u32[]{:S(2)}) collective-permute-start(bf16[16,1024]{1,0:T(8,128)(2,1)S(1)} %far_sent.1), channel_id=1, source_target_pairs={{0,4},{4,0},{8,12},{12,8},{16,20},{20,16},{24,28},{28,24},{32,36},... | collective-permute-start | bytes 98312 | tf_op jit(solution)/shard_map/ppermute | solution.py:230
  20.6 0.0 collective-permute-done.4.refs_3_
  20.6 0.0 collective-permute-done.3.refs_2_
  20.6 0.0 copy-done.1
  20.6 0.8 level.10
  21.4 2.8 %collective-permute-start.6 = (bf16[32,1024]{1,0:T(8,128)(2,1)S(1)}, bf16[32,1024]{1,0:T(8,128)(2,1)S(1)}, u32[]{:S(2)}, u32[]{:S(2)}) collective-permute-start(bf16[32,1024]{1,0:T(8,128)(2,1)S(1)} %get-tuple-element.88), channel_id=1, source_target_pairs={{0,8},{4,12},{8,0},{12,4},{16,24},{20,28},{24,16},{28,20},{32,40},... | collective-permute-start | bytes 196616 | tf_op jit(solution)/shard_map/ppermute | solution.py:230
  24.2 0.4 kept.10.refs_0_
  24.6 0.0 collective-permute-done.5.refs_3_
  24.6 0.8 level.11
  25.4 1.5 %collective-permute-start.7 = (bf16[32,1024]{1,0:T(8,128)(2,1)S(1)}, bf16[32,1024]{1,0:T(8,128)(2,1)S(1)}, u32[]{:S(2)}, u32[]{:S(2)}) collective-permute-start(bf16[32,1024]{1,0:T(8,128)(2,1)S(1)} %get-tuple-element.95), channel_id=1, source_target_pairs={{0,8},{4,12},{8,0},{12,4},{16,24},{20,28},{24,16},{28,20},{32,40},... | collective-permute-start | bytes 196616 | tf_op jit(solution)/shard_map/ppermute | solution.py:230
  26.9 0.4 kept.11.refs_0_
  27.3 0.6 collective-permute-done.6.refs_1_
  27.9 0.8 level.12
  28.7 0.1 collective-permute-start.8
  28.8 0.4 kept.12.refs_0_
  29.2 2.0 %collective-permute-done.7.refs_1_ = bf16[32,1024]{1,0:T(8,128)(2,1)S(1)} collective-permute-done((bf16[32,1024]{1,0:T(8,128)(2,1)S(1)}, bf16[32,1024]{1,0:T(8,128)(2,1)S(1)}, u32[]{:S(2)}, u32[]{:S(2)}) %collective-permute-start.7) | collective-permute-done | bytes 65568 | tf_op jit(solution)/shard_map/ppermute | solution.py:230
  31.2 0.8 level.13
  32.0 0.4 collective-permute-start.9
  32.4 0.4 kept.13.refs_0_
  32.8 0.3 collective-permute-done.8.refs_1_
  33.1 0.8 level.14
  33.8 1.7 %collective-permute-start.10 = (bf16[32,1024]{1,0:T(8,128)(2,1)S(1)}, bf16[32,1024]{1,0:T(8,128)(2,1)S(1)}, u32[]{:S(2)}, u32[]{:S(2)}) collective-permute-start(bf16[32,1024]{1,0:T(8,128)(2,1)S(1)} %get-tuple-element.108), channel_id=1, source_target_pairs={{0,32},{4,36},{8,40},{12,44},{16,48},{20,52},{24,56},{28,60},{32,0... | collective-permute-start | bytes 196616 | tf_op jit(solution)/shard_map/ppermute | solution.py:230
  35.5 0.4 kept.14.refs_0_
  35.9 0.5 collective-permute-done.9.refs_1_
  36.4 0.8 level.15
  37.1 1.1 %collective-permute-start.11 = (bf16[32,1024]{1,0:T(8,128)(2,1)S(1)}, bf16[32,1024]{1,0:T(8,128)(2,1)S(1)}, u32[]{:S(2)}, u32[]{:S(2)}) collective-permute-start(bf16[32,1024]{1,0:T(8,128)(2,1)S(1)} %get-tuple-element.115), channel_id=1, source_target_pairs={{0,32},{4,36},{8,40},{12,44},{16,48},{20,52},{24,56},{28,60},{32,0... | collective-permute-start | bytes 196616 | tf_op jit(solution)/shard_map/ppermute | solution.py:230
  38.3 0.4 kept.15.refs_0_
  38.7 0.5 collective-permute-done.10.refs_1_
  39.2 0.8 level.16
  40.0 1.7 %collective-permute-start.12 = (bf16[32,1024]{1,0:T(8,128)(2,1)S(1)}, bf16[32,1024]{1,0:T(8,128)(2,1)S(1)}, u32[]{:S(2)}, u32[]{:S(2)}) collective-permute-start(bf16[32,1024]{1,0:T(8,128)(2,1)S(1)} %get-tuple-element.118), channel_id=1, source_target_pairs={{0,64},{4,68},{8,72},{12,76},{16,80},{20,84},{24,88},{28,92},{32,9... | collective-permute-start | bytes 196616 | tf_op jit(solution)/shard_map/ppermute | solution.py:230
  41.6 0.4 kept.16.refs_0_
  42.0 0.7 collective-permute-done.11.refs_1_
  42.7 0.8 level.17
  43.5 1.7 %collective-permute-start.13 = (bf16[32,1024]{1,0:T(8,128)(2,1)S(1)}, bf16[32,1024]{1,0:T(8,128)(2,1)S(1)}, u32[]{:S(2)}, u32[]{:S(2)}) collective-permute-start(bf16[32,1024]{1,0:T(8,128)(2,1)S(1)} %get-tuple-element.125), channel_id=1, source_target_pairs={{0,64},{4,68},{8,72},{12,76},{16,80},{20,84},{24,88},{28,92},{32,9... | collective-permute-start | bytes 196616 | tf_op jit(solution)/shard_map/ppermute | solution.py:230
  45.1 0.4 kept.17.refs_0_
  45.5 0.0 collective-permute-done.12.refs_1_
  45.5 0.8 level.18
  46.3 0.4 kept.18.kept_ref
  46.7 3.0 %collective-permute-start.14 = (bf16[32,1024]{1,0:T(8,128)(2,1)S(1)}, bf16[32,1024]{1,0:T(8,128)(2,1)S(1)}, u32[]{:S(2)}, u32[]{:S(2)}) collective-permute-start(bf16[32,1024]{1,0:T(8,128)(2,1)S(1)} %get-tuple-element.128), channel_id=1, source_target_pairs={{0,128},{4,132},{8,136},{12,140},{16,144},{20,148},{24,152},{28,15... | collective-permute-start | bytes 196616 | tf_op jit(solution)/shard_map/ppermute | solution.py:230
  49.7 0.0 collective-permute-done.13.refs_1_
  49.7 0.8 level.19
  50.4 1.4 %collective-permute-start.15 = (bf16[32,1024]{1,0:T(8,128)(2,1)S(1)}, bf16[32,1024]{1,0:T(8,128)(2,1)S(1)}, u32[]{:S(2)}, u32[]{:S(2)}) collective-permute-start(bf16[32,1024]{1,0:T(8,128)(2,1)S(1)} %get-tuple-element.134), channel_id=1, source_target_pairs={{0,128},{4,132},{8,136},{12,140},{16,144},{20,148},{24,152},{28,15... | collective-permute-start | bytes 196616 | tf_op jit(solution)/shard_map/ppermute | solution.py:230
  51.9 0.4 kept.19.kept_ref
  52.2 0.3 collective-permute-done.14.got_ref
  52.5 0.5 last.2
  53.0 3.3 %collective-permute-done.15.got_ref = bf16[32,1024]{1,0:T(8,128)(2,1)S(1)} collective-permute-done((bf16[32,1024]{1,0:T(8,128)(2,1)S(1)}, bf16[32,1024]{1,0:T(8,128)(2,1)S(1)}, u32[]{:S(2)}, u32[]{:S(2)}) %collective-permute-start.15) | collective-permute-done | bytes 65568 | tf_op jit(solution)/shard_map/ppermute | solution.py:230
  56.3 0.0 collective-permute-start.16
  56.3 0.5 last.3.same_ref
  56.8 0.8 collective-permute-done.16.other_ref
  57.6 0.1 merge.1
  57.7 24.5 %all_to_all.5 = bf16[128,8,128]{2,1,0:T(8,128)(2,1)S(1)} all-to-all(bf16[128,8,128]{2,1,0:T(8,128)(2,1)S(1)} %merge.1), channel_id=1, replica_groups=mesh['pts'=64,'h'=2,'c'=2] {'pts','h'}, dimensions={0} | all-to-all | bytes 524288 | tf_op jit(solution)/shard_map/all_to_all | solution.py:281
  82.2 1.2 %finish.1 = bf16[2,8,8192]{2,1,0:T(8,128)(2,1)} custom-call(bf16[1024,128]{1,0:T(8,128)(2,1)S(1)} %bitcast.1), custom_call_target="tpu_custom_call" | custom-call | flops 1 | bytes 1 | tf_op jit(solution)/shard_map/finish/pallas_call | solution.py:212
  (6 shorter events, 0.0 us)
Async XLA Ops:
  0.0 0.8 %copy-start = (s32[6,2048]{1,0:T(8,128)S(1)}, s32[6,2048]{1,0:T(8,128)}, u32[]{:S(2)}) copy-start(s32[6,2048]{1,0:T(8,128)} %order_ref.21) | copy-start | bytes 147460
  0.8 0.9 %copy-start.2 = (bf16[2,8,8192]{2,1,0:T(8,128)(2,1)S(1)}, bf16[2,8,8192]{2,1,0:T(8,128)(2,1)}, u32[]{:S(2)}) copy-start(bf16[2,8,8192]{2,1,0:T(8,128)(2,1)} %x_ref.1) | copy-start | bytes 786436
  1.8 18.8 %copy-start.1 = (s32[6,2048]{1,0:T(8,128)S(1)}, s32[6,2048]{1,0:T(8,128)}, u32[]{:S(2)}) copy-start(s32[6,2048]{1,0:T(8,128)} %order_ref.21) | copy-start | bytes 147460
  3.0 6.5 %collective-permute-start = (bf16[32,1024]{1,0:T(8,128)(2,1)S(1)}, bf16[32,1024]{1,0:T(8,128)(2,1)S(1)}, u32[]{:S(2)}, u32[]{:S(2)}) collective-permute-start(bf16[32,1024]{1,0:T(8,128)(2,1)S(1)} %get-tuple-element.73), channel_id=1, source_target_pairs={{0,1},{1,0},{2,3},{3,2},{4,5},{5,4},{6,7},{7,6},{8,9},{9,8},{10,11... | collective-permute-start | bytes 196616 | tf_op jit(solution)/shard_map/ppermute | solution.py:234
  3.1 11.4 %collective-permute-start.2 = (bf16[32,1024]{1,0:T(8,128)(2,1)S(1)}, bf16[32,1024]{1,0:T(8,128)(2,1)S(1)}, u32[]{:S(2)}, u32[]{:S(2)}) collective-permute-start(bf16[32,1024]{1,0:T(8,128)(2,1)S(1)} %get-tuple-element.78), channel_id=1, source_target_pairs={{0,3},{1,2},{2,1},{3,0},{4,7},{5,6},{6,5},{7,4},{8,11},{9,10},{10,... | collective-permute-start | bytes 196616 | tf_op jit(solution)/shard_map/ppermute | solution.py:234
  9.5 9.6 %collective-permute-start.1 = (bf16[32,1024]{1,0:T(8,128)(2,1)S(1)}, bf16[32,1024]{1,0:T(8,128)(2,1)S(1)}, u32[]{:S(2)}, u32[]{:S(2)}) collective-permute-start(bf16[32,1024]{1,0:T(8,128)(2,1)S(1)} %get-tuple-element.75), channel_id=1, source_target_pairs={{0,2},{2,0},{1,3},{3,1},{4,6},{6,4},{5,7},{7,5},{8,10},{10,8},{9,1... | collective-permute-start | bytes 196616 | tf_op jit(solution)/shard_map/ppermute | solution.py:234
  10.7 10.0 %collective-permute-start.3 = (bf16[32,1024]{1,0:T(8,128)(2,1)S(1)}, bf16[32,1024]{1,0:T(8,128)(2,1)S(1)}, u32[]{:S(2)}, u32[]{:S(2)}) collective-permute-start(bf16[32,1024]{1,0:T(8,128)(2,1)S(1)} %near.1), channel_id=1, source_target_pairs={{0,4},{4,0},{8,12},{12,8},{16,20},{20,16},{24,28},{28,24},{32,36},... | collective-permute-start | bytes 196616 | tf_op jit(solution)/shard_map/ppermute | solution.py:230
  14.6 6.0 %collective-permute-start.4 = (bf16[16,1024]{1,0:T(8,128)(2,1)S(1)}, bf16[16,1024]{1,0:T(8,128)(2,1)S(1)}, u32[]{:S(2)}, u32[]{:S(2)}) collective-permute-start(bf16[16,1024]{1,0:T(8,128)(2,1)S(1)} %core_sent.1), channel_id=1, source_target_pairs={{0,4},{4,0},{8,12},{12,8},{16,20},{20,16},{24,28},{28,24},{32,36},... | collective-permute-start | bytes 98312 | tf_op jit(solution)/shard_map/ppermute | solution.py:230
  19.1 5.5 %collective-permute-start.5 = (bf16[16,1024]{1,0:T(8,128)(2,1)S(1)}, bf16[16,1024]{1,0:T(8,128)(2,1)S(1)}, u32[]{:S(2)}, u32[]{:S(2)}) collective-permute-start(bf16[16,1024]{1,0:T(8,128)(2,1)S(1)} %far_sent.1), channel_id=1, source_target_pairs={{0,4},{4,0},{8,12},{12,8},{16,20},{20,16},{24,28},{28,24},{32,36},... | collective-permute-start | bytes 98312 | tf_op jit(solution)/shard_map/ppermute | solution.py:230
  21.4 6.5 %collective-permute-start.6 = (bf16[32,1024]{1,0:T(8,128)(2,1)S(1)}, bf16[32,1024]{1,0:T(8,128)(2,1)S(1)}, u32[]{:S(2)}, u32[]{:S(2)}) collective-permute-start(bf16[32,1024]{1,0:T(8,128)(2,1)S(1)} %get-tuple-element.88), channel_id=1, source_target_pairs={{0,8},{4,12},{8,0},{12,4},{16,24},{20,28},{24,16},{28,20},{32,40},... | collective-permute-start | bytes 196616 | tf_op jit(solution)/shard_map/ppermute | solution.py:230
  25.4 5.9 %collective-permute-start.7 = (bf16[32,1024]{1,0:T(8,128)(2,1)S(1)}, bf16[32,1024]{1,0:T(8,128)(2,1)S(1)}, u32[]{:S(2)}, u32[]{:S(2)}) collective-permute-start(bf16[32,1024]{1,0:T(8,128)(2,1)S(1)} %get-tuple-element.95), channel_id=1, source_target_pairs={{0,8},{4,12},{8,0},{12,4},{16,24},{20,28},{24,16},{28,20},{32,40},... | collective-permute-start | bytes 196616 | tf_op jit(solution)/shard_map/ppermute | solution.py:230
  28.7 4.4 %collective-permute-start.8 = (bf16[32,1024]{1,0:T(8,128)(2,1)S(1)}, bf16[32,1024]{1,0:T(8,128)(2,1)S(1)}, u32[]{:S(2)}, u32[]{:S(2)}) collective-permute-start(bf16[32,1024]{1,0:T(8,128)(2,1)S(1)} %get-tuple-element.98), channel_id=1, source_target_pairs={{0,16},{4,20},{8,24},{12,28},{16,0},{20,4},{24,8},{28,12},{32,48},... | collective-permute-start | bytes 196616 | tf_op jit(solution)/shard_map/ppermute | solution.py:230
  32.0 4.4 %collective-permute-start.9 = (bf16[32,1024]{1,0:T(8,128)(2,1)S(1)}, bf16[32,1024]{1,0:T(8,128)(2,1)S(1)}, u32[]{:S(2)}, u32[]{:S(2)}) collective-permute-start(bf16[32,1024]{1,0:T(8,128)(2,1)S(1)} %get-tuple-element.105), channel_id=1, source_target_pairs={{0,16},{4,20},{8,24},{12,28},{16,0},{20,4},{24,8},{28,12},{32,48},... | collective-permute-start | bytes 196616 | tf_op jit(solution)/shard_map/ppermute | solution.py:230
  33.8 5.4 %collective-permute-start.10 = (bf16[32,1024]{1,0:T(8,128)(2,1)S(1)}, bf16[32,1024]{1,0:T(8,128)(2,1)S(1)}, u32[]{:S(2)}, u32[]{:S(2)}) collective-permute-start(bf16[32,1024]{1,0:T(8,128)(2,1)S(1)} %get-tuple-element.108), channel_id=1, source_target_pairs={{0,32},{4,36},{8,40},{12,44},{16,48},{20,52},{24,56},{28,60},{32,0... | collective-permute-start | bytes 196616 | tf_op jit(solution)/shard_map/ppermute | solution.py:230
  37.1 5.5 %collective-permute-start.11 = (bf16[32,1024]{1,0:T(8,128)(2,1)S(1)}, bf16[32,1024]{1,0:T(8,128)(2,1)S(1)}, u32[]{:S(2)}, u32[]{:S(2)}) collective-permute-start(bf16[32,1024]{1,0:T(8,128)(2,1)S(1)} %get-tuple-element.115), channel_id=1, source_target_pairs={{0,32},{4,36},{8,40},{12,44},{16,48},{20,52},{24,56},{28,60},{32,0... | collective-permute-start | bytes 196616 | tf_op jit(solution)/shard_map/ppermute | solution.py:230
  40.0 5.5 %collective-permute-start.12 = (bf16[32,1024]{1,0:T(8,128)(2,1)S(1)}, bf16[32,1024]{1,0:T(8,128)(2,1)S(1)}, u32[]{:S(2)}, u32[]{:S(2)}) collective-permute-start(bf16[32,1024]{1,0:T(8,128)(2,1)S(1)} %get-tuple-element.118), channel_id=1, source_target_pairs={{0,64},{4,68},{8,72},{12,76},{16,80},{20,84},{24,88},{28,92},{32,9... | collective-permute-start | bytes 196616 | tf_op jit(solution)/shard_map/ppermute | solution.py:230
  43.5 6.2 %collective-permute-start.13 = (bf16[32,1024]{1,0:T(8,128)(2,1)S(1)}, bf16[32,1024]{1,0:T(8,128)(2,1)S(1)}, u32[]{:S(2)}, u32[]{:S(2)}) collective-permute-start(bf16[32,1024]{1,0:T(8,128)(2,1)S(1)} %get-tuple-element.125), channel_id=1, source_target_pairs={{0,64},{4,68},{8,72},{12,76},{16,80},{20,84},{24,88},{28,92},{32,9... | collective-permute-start | bytes 196616 | tf_op jit(solution)/shard_map/ppermute | solution.py:230
  46.7 5.9 %collective-permute-start.14 = (bf16[32,1024]{1,0:T(8,128)(2,1)S(1)}, bf16[32,1024]{1,0:T(8,128)(2,1)S(1)}, u32[]{:S(2)}, u32[]{:S(2)}) collective-permute-start(bf16[32,1024]{1,0:T(8,128)(2,1)S(1)} %get-tuple-element.128), channel_id=1, source_target_pairs={{0,128},{4,132},{8,136},{12,140},{16,144},{20,148},{24,152},{28,15... | collective-permute-start | bytes 196616 | tf_op jit(solution)/shard_map/ppermute | solution.py:230
  50.4 5.9 %collective-permute-start.15 = (bf16[32,1024]{1,0:T(8,128)(2,1)S(1)}, bf16[32,1024]{1,0:T(8,128)(2,1)S(1)}, u32[]{:S(2)}, u32[]{:S(2)}) collective-permute-start(bf16[32,1024]{1,0:T(8,128)(2,1)S(1)} %get-tuple-element.134), channel_id=1, source_target_pairs={{0,128},{4,132},{8,136},{12,140},{16,144},{20,148},{24,152},{28,15... | collective-permute-start | bytes 196616 | tf_op jit(solution)/shard_map/ppermute | solution.py:230
  56.3 1.3 %collective-permute-start.16 = (bf16[64,8,128]{2,1,0:T(8,128)(2,1)S(1)}, bf16[64,8,128]{2,1,0:T(8,128)(2,1)S(1)}, u32[]{:S(2)}, u32[]{:S(2)}) collective-permute-start(bf16[64,8,128]{2,1,0:T(8,128)(2,1)S(1)} %last.2), channel_id=1, source_target_pairs={{0,1},{1,0},{2,3},{3,2},{4,5},{5,4},{6,7},{7,6},{8,9},{9,8},{10,11... | collective-permute-start | bytes 393224 | tf_op jit(solution)/shard_map/ppermute | solution.py:234

commit v3 on v2

--- a/solution.py
+++ b/solution.py
@@ -32,21 +32,26 @@
     )
 
 
+def gather_columns(sources, index, count):
+    lane = (index % LANES).astype(jnp.int16)
+    which = (index // LANES).astype(jnp.int16)
+    picked = [None] * len(sources)
+    for s in range(count):
+        here = which == jnp.int16(s)
+        for g, source in enumerate(sources):
+            value = take_lanes(source(s), lane)
+            picked[g] = value if s == 0 else jnp.where(here, value, picked[g])
+    return picked
+
+
 def gather_half(sources, order_ref, level, start, targets):
     half = order_ref.shape[1] // 2
     for t in range(half // LANES):
         columns = pl.ds(pl.multiple_of(start + t * LANES, LANES), LANES)
         index = jnp.broadcast_to(order_ref[level : level + 1, columns], (TILE, LANES))
-        lane = (index % LANES).astype(jnp.int16)
-        which = (index // LANES).astype(jnp.int16)
-        picked = [None] * len(sources)
-        for s in range(2 * half // LANES):
-            here = which == jnp.int16(s)
-            for g, source in enumerate(sources):
-                value = take_lanes(source(s), lane)
-                picked[g] = value if s == 0 else jnp.where(here, value, picked[g])
-        for g, (ref, row) in enumerate(targets):
-            ref[row : row + TILE, t * LANES : (t + 1) * LANES] = picked[g]
+        values = gather_columns(sources, index, 2 * half // LANES)
+        for (ref, row), value in zip(targets, values):
+            ref[row : row + TILE, t * LANES : (t + 1) * LANES] = value
 
 
 def turned(tile):
@@ -84,8 +89,11 @@
         copy.wait()
 
 
-def start_kernel(x_ref, order_ref, *outs):
-    upper = upper_half(0)
+def side_kernel(side_out):
+    side_out[...] = jnp.full(side_out.shape, upper_half(0), jnp.int32)
+
+
+def start_kernel(x_ref, order_ref, side_ref, *outs):
     zhi, core = lax.axis_index("h"), lax.axis_index("c")
     rows = order_ref.shape[1]
     half = rows // 2
@@ -103,8 +111,14 @@
         columns(zhi, core), columns(1 - zhi, core), columns(zhi, 1 - core), columns(1 - zhi, 1 - core),
     ]
     sources = [lambda s, g=g: g[s] for g in groups]
-    gather_half(sources, order_ref, 0, upper * half, [(out, 0) for out in outs])
-    gather_half(sources, order_ref, 0, (1 - upper) * half, [(out, TILE) for out in outs])
+    upper = side_ref[...] == 1
+    for t in range(half // LANES):
+        low, high = (
+            jnp.broadcast_to(order_ref[0:1, at : at + LANES], (TILE, LANES)) for at in (t * LANES, half + t * LANES)
+        )
+        for row, index in ((0, jnp.where(upper, high, low)), (TILE, jnp.where(upper, low, high))):
+            for out, value in zip(outs, gather_columns(sources, index, rows // LANES)):
+                out[row : row + TILE, t * LANES : (t + 1) * LANES] = value
 
 
 def tiles_of(refs, rows):
@@ -233,8 +247,9 @@
         count = 2 ** len(names)
         return lax.ppermute(value, names, [(i, count - 1 - i) for i in range(count)])
 
+    side = run("side", side_kernel, (), jax.ShapeDtypeStruct((TILE, LANES), jnp.int32), flops=1 << 33)
     near, far, core_near, core_far = run(
-        "start", start_kernel, (probe_vectors, row_orders), [bf16(2 * TILE, half)] * 4
+        "start", start_kernel, (probe_vectors, row_orders, side), [bf16(2 * TILE, half)] * 4
     )
     core_far = over(core_far, ("h", "c"))
     core_near = over(core_near, "c")
@@ -269,14 +284,12 @@
     def last(which, kept, got):
         return run(
             "last", functools.partial(last_kernel, which == 0),
-            (*kept, *got, *layers[2 * LEVELS - 2 :]), bf16(pts, 8, LANES),
+            (*kept, *got, *layers[2 * LEVELS - 2 :]), bf16(pts, 8, LANES), flops=1 << 33,
         )
 
     other = last(0, *chains[0])
-    kept, got = chains[1]
-    other, got = lax.optimization_barrier((other, got))
     other = over(other, "c")
-    same = last(1, kept, got)
+    same = last(1, *chains[1])
     outgoing = run("merge", merge_kernel, (same, other), bf16(2 * pts, 8, LANES))
     arrived = lax.all_to_all(outgoing, ("pts", "h"), 0, 0, tiled=True)
     return run(

time: 83.6 us -> 81.7 us (0.977)
  waiting for transfers between devices: 11.7 us -> 10.3 us
    unnamed x6 -> x4, local copies, waits for them, and re-layouts: 1.79 us -> 0.98 us
    pallas_call x29 -> x30, Pallas kernels: 17.9 us -> 17.9 us  [run(): pl.pallas_call(kernel, out_shape=outs, in_specs=[space] * len(operands),...]
  transfers between devices with their start and end apart: 17 -> 17, of which waited for: 11 -> 9; matrix products, arithmetic and copies ran while one was open for 0% -> 0% of each run, Pallas kernels for 18% -> 19%
where the time goes in v3:
time: 81.7 us; the launch traced here: 81.5 us
  starting transfers between devices  27.8 us (34%)
  blocking collectives  24.5 us (30%)
  Pallas kernels  17.9 us (22%)
  waiting for transfers between devices  10.3 us (13%)
  local copies, waits for them, and re-layouts  0.98 us (1%)
    all_to_all x1, blocking collectives, local(): arrived = lax.all_to_all(outgoing, ('pts', 'h'), 0, 0, tiled=True)  24.5 us
    ppermute x13, starting transfers between devices, across(): return lax.ppermute(value, 'pts', [(i, i ^ 1 << bit) for i in range(pts)])  20 us
    pallas_call x30, Pallas kernels, run(): pl.pallas_call(kernel, out_shape=outs, in_specs=[space] * len(operands),...  17.9 us
    ppermute x4, starting transfers between devices, over(): lax.ppermute(value, names, [(i, count - 1 - i) for i in range(count)])  7.71 us
    ppermute x13, waiting for transfers between devices, across(): return lax.ppermute(value, 'pts', [(i, i ^ 1 << bit) for i in range(pts)])  7.7 us
    ppermute x4, waiting for transfers between devices, over(): lax.ppermute(value, names, [(i, count - 1 - i) for i in range(count)])  2.59 us
  transfers between devices with their start and end apart: 17, of which 9 were waited for; matrix products, arithmetic and copies ran while one was open for 0% of the time, Pallas kernels for 19%

profile of v3, /device:TPU:32, one launch (start us, length us, event | category | flops | bytes accessed | tf_op | source)
XLA Modules:
  0.0 81.5 jit_solution(15100823253231692185)
XLA Ops:
  0.0 0.0 copy-start
  0.0 0.8 %copy-done = s32[6,2048]{1,0:T(8,128)S(1)} copy-done((s32[6,2048]{1,0:T(8,128)S(1)}, s32[6,2048]{1,0:T(8,128)}, u32[]{:S(2)}) %copy-start) | copy-done | bytes 49176
  0.8 0.1 copy-done.1
  1.0 1.2 %start.1 = (bf16[32,1024]{1,0:T(8,128)(2,1)S(1)}, bf16[32,1024]{1,0:T(8,128)(2,1)S(1)}, bf16[32,1024]{1,0:T(8,128)(2,1)S(1)}, bf16[32,1024]{1,0:T(8,128)(2,1)S(1)}) custom-call(bf16[2,8,8192]{2,1,0:T(8,128)(2,1)S(1)} %copy-done.1, s32[6,2048]{1,0:T(8,128)S(1)} %copy-done, s32[16,128]{1,0:T(8,128)S(1)} %side.1.side_ref), custom_call_target="tpu_custom_call" | custom-call | flops 1 | bytes 1 | tf_op jit(solution)/shard_map/start/pallas_call | solution.py:226
  2.2 0.1 collective-permute-start
  2.3 6.4 %collective-permute-start.2 = (bf16[32,1024]{1,0:T(8,128)(2,1)S(1)}, bf16[32,1024]{1,0:T(8,128)(2,1)S(1)}, u32[]{:S(2)}, u32[]{:S(2)}) collective-permute-start(bf16[32,1024]{1,0:T(8,128)(2,1)S(1)} %get-tuple-element.76), channel_id=1, source_target_pairs={{0,3},{1,2},{2,1},{3,0},{4,7},{5,6},{6,5},{7,4},{8,11},{9,10},{10,... | collective-permute-start | bytes 196616 | tf_op jit(solution)/shard_map/ppermute | solution.py:248
  8.7 0.0 collective-permute-done.core_ref.refs_0_
  8.7 1.1 %collective-permute-start.1 = (bf16[32,1024]{1,0:T(8,128)(2,1)S(1)}, bf16[32,1024]{1,0:T(8,128)(2,1)S(1)}, u32[]{:S(2)}, u32[]{:S(2)}) collective-permute-start(bf16[32,1024]{1,0:T(8,128)(2,1)S(1)} %get-tuple-element.73), channel_id=1, source_target_pairs={{0,2},{2,0},{1,3},{3,1},{4,6},{6,4},{5,7},{7,5},{8,10},{10,8},{9,1... | collective-permute-start | bytes 196616 | tf_op jit(solution)/shard_map/ppermute | solution.py:248
  9.8 1.5 %collective-permute-start.3 = (bf16[32,1024]{1,0:T(8,128)(2,1)S(1)}, bf16[32,1024]{1,0:T(8,128)(2,1)S(1)}, u32[]{:S(2)}, u32[]{:S(2)}) collective-permute-start(bf16[32,1024]{1,0:T(8,128)(2,1)S(1)} %near.1), channel_id=1, source_target_pairs={{0,4},{4,0},{8,12},{12,8},{16,20},{20,16},{24,28},{28,24},{32,36},... | collective-permute-start | bytes 196616 | tf_op jit(solution)/shard_map/ppermute | solution.py:244
  11.3 2.4 %collective-permute-done.2.ref.refs_1_ = bf16[32,1024]{1,0:T(8,128)(2,1)S(1)} collective-permute-done((bf16[32,1024]{1,0:T(8,128)(2,1)S(1)}, bf16[32,1024]{1,0:T(8,128)(2,1)S(1)}, u32[]{:S(2)}, u32[]{:S(2)}) %collective-permute-start.2) | collective-permute-done | bytes 65568 | tf_op jit(solution)/shard_map/ppermute | solution.py:248
  13.7 1.5 %collective-permute-start.4 = (bf16[16,1024]{1,0:T(8,128)(2,1)S(1)}, bf16[16,1024]{1,0:T(8,128)(2,1)S(1)}, u32[]{:S(2)}, u32[]{:S(2)}) collective-permute-start(bf16[16,1024]{1,0:T(8,128)(2,1)S(1)} %core_sent.1), channel_id=1, source_target_pairs={{0,4},{4,0},{8,12},{12,8},{16,20},{20,16},{24,28},{28,24},{32,36},... | collective-permute-start | bytes 98312 | tf_op jit(solution)/shard_map/ppermute | solution.py:244
  15.2 2.9 %fetch.1 = (bf16[2048,128]{1,0:T(8,128)(2,1)S(1)}, bf16[2048,128]{1,0:T(8,128)(2,1)S(1)}, bf16[2048,128]{1,0:T(8,128)(2,1)S(1)}, bf16[2048,128]{1,0:T(8,128)(2,1...) custom-call(bf16[6,2,2048,128]{3,2,1,0:T(8,128)(2,1)} %f_hbm), custom_call_target="tpu_custom_call" | custom-call | flops 1 | bytes 1 | tf_op jit(solution)/shard_map/fetch/pallas_call | solution.py:226
  18.1 0.2 collective-permute-done.1.ref.refs_1_
  18.3 1.5 %collective-permute-start.5 = (bf16[16,1024]{1,0:T(8,128)(2,1)S(1)}, bf16[16,1024]{1,0:T(8,128)(2,1)S(1)}, u32[]{:S(2)}, u32[]{:S(2)}) collective-permute-start(bf16[16,1024]{1,0:T(8,128)(2,1)S(1)} %far_sent.1), channel_id=1, source_target_pairs={{0,4},{4,0},{8,12},{12,8},{16,20},{20,16},{24,28},{28,24},{32,36},... | collective-permute-start | bytes 98312 | tf_op jit(solution)/shard_map/ppermute | solution.py:244
  19.8 0.0 collective-permute-done.4.refs_3_
  19.8 0.0 collective-permute-done.3.refs_2_
  19.8 0.8 level.10
  20.6 2.8 %collective-permute-start.6 = (bf16[32,1024]{1,0:T(8,128)(2,1)S(1)}, bf16[32,1024]{1,0:T(8,128)(2,1)S(1)}, u32[]{:S(2)}, u32[]{:S(2)}) collective-permute-start(bf16[32,1024]{1,0:T(8,128)(2,1)S(1)} %get-tuple-element.86), channel_id=1, source_target_pairs={{0,8},{4,12},{8,0},{12,4},{16,24},{20,28},{24,16},{28,20},{32,40},... | collective-permute-start | bytes 196616 | tf_op jit(solution)/shard_map/ppermute | solution.py:244
  23.4 0.4 kept.10.refs_0_
  23.8 0.0 collective-permute-done.5.refs_3_
  23.8 0.8 level.11
  24.5 1.6 %collective-permute-start.7 = (bf16[32,1024]{1,0:T(8,128)(2,1)S(1)}, bf16[32,1024]{1,0:T(8,128)(2,1)S(1)}, u32[]{:S(2)}, u32[]{:S(2)}) collective-permute-start(bf16[32,1024]{1,0:T(8,128)(2,1)S(1)} %get-tuple-element.93), channel_id=1, source_target_pairs={{0,8},{4,12},{8,0},{12,4},{16,24},{20,28},{24,16},{28,20},{32,40},... | collective-permute-start | bytes 196616 | tf_op jit(solution)/shard_map/ppermute | solution.py:244
  26.1 0.4 kept.11.refs_0_
  26.5 0.6 collective-permute-done.6.refs_1_
  27.1 0.8 level.12
  27.9 0.1 collective-permute-start.8
  28.0 0.4 kept.12.refs_0_
  28.4 2.0 %collective-permute-done.7.refs_1_ = bf16[32,1024]{1,0:T(8,128)(2,1)S(1)} collective-permute-done((bf16[32,1024]{1,0:T(8,128)(2,1)S(1)}, bf16[32,1024]{1,0:T(8,128)(2,1)S(1)}, u32[]{:S(2)}, u32[]{:S(2)}) %collective-permute-start.7) | collective-permute-done | bytes 65568 | tf_op jit(solution)/shard_map/ppermute | solution.py:244
  30.4 0.8 level.13
  31.2 0.4 collective-permute-start.9
  31.6 0.4 kept.13.refs_0_
  31.9 0.3 collective-permute-done.8.refs_1_
  32.2 0.8 level.14
  33.0 1.8 %collective-permute-start.10 = (bf16[32,1024]{1,0:T(8,128)(2,1)S(1)}, bf16[32,1024]{1,0:T(8,128)(2,1)S(1)}, u32[]{:S(2)}, u32[]{:S(2)}) collective-permute-start(bf16[32,1024]{1,0:T(8,128)(2,1)S(1)} %get-tuple-element.106), channel_id=1, source_target_pairs={{0,32},{4,36},{8,40},{12,44},{16,48},{20,52},{24,56},{28,60},{32,0... | collective-permute-start | bytes 196616 | tf_op jit(solution)/shard_map/ppermute | solution.py:244
  34.8 0.4 kept.14.refs_0_
  35.2 0.3 collective-permute-done.9.refs_1_
  35.5 0.8 level.15
  36.3 1.1 %collective-permute-start.11 = (bf16[32,1024]{1,0:T(8,128)(2,1)S(1)}, bf16[32,1024]{1,0:T(8,128)(2,1)S(1)}, u32[]{:S(2)}, u32[]{:S(2)}) collective-permute-start(bf16[32,1024]{1,0:T(8,128)(2,1)S(1)} %get-tuple-element.113), channel_id=1, source_target_pairs={{0,32},{4,36},{8,40},{12,44},{16,48},{20,52},{24,56},{28,60},{32,0... | collective-permute-start | bytes 196616 | tf_op jit(solution)/shard_map/ppermute | solution.py:244
  37.5 0.4 kept.15.refs_0_
  37.8 0.7 collective-permute-done.10.refs_1_
  38.5 0.8 level.16
  39.3 1.7 %collective-permute-start.12 = (bf16[32,1024]{1,0:T(8,128)(2,1)S(1)}, bf16[32,1024]{1,0:T(8,128)(2,1)S(1)}, u32[]{:S(2)}, u32[]{:S(2)}) collective-permute-start(bf16[32,1024]{1,0:T(8,128)(2,1)S(1)} %get-tuple-element.116), channel_id=1, source_target_pairs={{0,64},{4,68},{8,72},{12,76},{16,80},{20,84},{24,88},{28,92},{32,9... | collective-permute-start | bytes 196616 | tf_op jit(solution)/shard_map/ppermute | solution.py:244
  41.0 0.4 kept.16.refs_0_
  41.4 0.3 collective-permute-done.11.refs_1_
  41.6 0.8 level.17
  42.4 1.7 %collective-permute-start.13 = (bf16[32,1024]{1,0:T(8,128)(2,1)S(1)}, bf16[32,1024]{1,0:T(8,128)(2,1)S(1)}, u32[]{:S(2)}, u32[]{:S(2)}) collective-permute-start(bf16[32,1024]{1,0:T(8,128)(2,1)S(1)} %get-tuple-element.123), channel_id=1, source_target_pairs={{0,64},{4,68},{8,72},{12,76},{16,80},{20,84},{24,88},{28,92},{32,9... | collective-permute-start | bytes 196616 | tf_op jit(solution)/shard_map/ppermute | solution.py:244
  44.1 0.4 kept.17.refs_0_
  44.4 0.0 collective-permute-done.12.refs_1_
  44.4 0.8 level.18
  45.2 3.0 %collective-permute-start.14 = (bf16[32,1024]{1,0:T(8,128)(2,1)S(1)}, bf16[32,1024]{1,0:T(8,128)(2,1)S(1)}, u32[]{:S(2)}, u32[]{:S(2)}) collective-permute-start(bf16[32,1024]{1,0:T(8,128)(2,1)S(1)} %get-tuple-element.126), channel_id=1, source_target_pairs={{0,128},{4,132},{8,136},{12,140},{16,144},{20,148},{24,152},{28,15... | collective-permute-start | bytes 196616 | tf_op jit(solution)/shard_map/ppermute | solution.py:244
  48.2 0.4 kept.18.kept_ref
  48.6 0.0 collective-permute-done.13.refs_1_
  48.6 0.8 level.19
  49.4 1.4 %collective-permute-start.15 = (bf16[32,1024]{1,0:T(8,128)(2,1)S(1)}, bf16[32,1024]{1,0:T(8,128)(2,1)S(1)}, u32[]{:S(2)}, u32[]{:S(2)}) collective-permute-start(bf16[32,1024]{1,0:T(8,128)(2,1)S(1)} %get-tuple-element.128), channel_id=1, source_target_pairs={{0,128},{4,132},{8,136},{12,140},{16,144},{20,148},{24,152},{28,15... | collective-permute-start | bytes 196616 | tf_op jit(solution)/shard_map/ppermute | solution.py:244
  50.8 0.4 kept.19.kept_ref
  51.2 0.0 collective-permute-done.14.got_ref
  51.2 0.5 last.3
  51.7 0.1 collective-permute-start.16
  51.8 3.4 %collective-permute-done.15.got_ref = bf16[32,1024]{1,0:T(8,128)(2,1)S(1)} collective-permute-done((bf16[32,1024]{1,0:T(8,128)(2,1)S(1)}, bf16[32,1024]{1,0:T(8,128)(2,1)S(1)}, u32[]{:S(2)}, u32[]{:S(2)}) %collective-permute-start.15) | collective-permute-done | bytes 65568 | tf_op jit(solution)/shard_map/ppermute | solution.py:244
  55.2 0.5 last.2.same_ref
  55.7 0.0 collective-permute-done.16.other_ref
  55.7 0.1 merge.1
  55.8 24.5 %all_to_all.5 = bf16[128,8,128]{2,1,0:T(8,128)(2,1)S(1)} all-to-all(bf16[128,8,128]{2,1,0:T(8,128)(2,1)S(1)} %merge.1), channel_id=1, replica_groups=mesh['pts'=64,'h'=2,'c'=2] {'pts','h'}, dimensions={0} | all-to-all | bytes 524288 | tf_op jit(solution)/shard_map/all_to_all | solution.py:294
  80.3 1.2 %finish.1 = bf16[2,8,8192]{2,1,0:T(8,128)(2,1)} custom-call(bf16[1024,128]{1,0:T(8,128)(2,1)S(1)} %bitcast.1), custom_call_target="tpu_custom_call" | custom-call | flops 1 | bytes 1 | tf_op jit(solution)/shard_map/finish/pallas_call | solution.py:226
  (5 shorter events, 0.0 us)
Async XLA Ops:
  0.0 0.8 %copy-start = (s32[6,2048]{1,0:T(8,128)S(1)}, s32[6,2048]{1,0:T(8,128)}, u32[]{:S(2)}) copy-start(s32[6,2048]{1,0:T(8,128)} %order_ref.21) | copy-start | bytes 147460
  0.0 1.0 %copy-start.1 = (bf16[2,8,8192]{2,1,0:T(8,128)(2,1)S(1)}, bf16[2,8,8192]{2,1,0:T(8,128)(2,1)}, u32[]{:S(2)}) copy-start(bf16[2,8,8192]{2,1,0:T(8,128)(2,1)} %x_ref.1) | copy-start | bytes 786436
  2.2 6.5 %collective-permute-start = (bf16[32,1024]{1,0:T(8,128)(2,1)S(1)}, bf16[32,1024]{1,0:T(8,128)(2,1)S(1)}, u32[]{:S(2)}, u32[]{:S(2)}) collective-permute-start(bf16[32,1024]{1,0:T(8,128)(2,1)S(1)} %get-tuple-element.71), channel_id=1, source_target_pairs={{0,1},{1,0},{2,3},{3,2},{4,5},{5,4},{6,7},{7,6},{8,9},{9,8},{10,11... | collective-permute-start | bytes 196616 | tf_op jit(solution)/shard_map/ppermute | solution.py:248
  2.3 11.4 %collective-permute-start.2 = (bf16[32,1024]{1,0:T(8,128)(2,1)S(1)}, bf16[32,1024]{1,0:T(8,128)(2,1)S(1)}, u32[]{:S(2)}, u32[]{:S(2)}) collective-permute-start(bf16[32,1024]{1,0:T(8,128)(2,1)S(1)} %get-tuple-element.76), channel_id=1, source_target_pairs={{0,3},{1,2},{2,1},{3,0},{4,7},{5,6},{6,5},{7,4},{8,11},{9,10},{10,... | collective-permute-start | bytes 196616 | tf_op jit(solution)/shard_map/ppermute | solution.py:248
  8.7 9.6 %collective-permute-start.1 = (bf16[32,1024]{1,0:T(8,128)(2,1)S(1)}, bf16[32,1024]{1,0:T(8,128)(2,1)S(1)}, u32[]{:S(2)}, u32[]{:S(2)}) collective-permute-start(bf16[32,1024]{1,0:T(8,128)(2,1)S(1)} %get-tuple-element.73), channel_id=1, source_target_pairs={{0,2},{2,0},{1,3},{3,1},{4,6},{6,4},{5,7},{7,5},{8,10},{10,8},{9,1... | collective-permute-start | bytes 196616 | tf_op jit(solution)/shard_map/ppermute | solution.py:248
  9.8 10.0 %collective-permute-start.3 = (bf16[32,1024]{1,0:T(8,128)(2,1)S(1)}, bf16[32,1024]{1,0:T(8,128)(2,1)S(1)}, u32[]{:S(2)}, u32[]{:S(2)}) collective-permute-start(bf16[32,1024]{1,0:T(8,128)(2,1)S(1)} %near.1), channel_id=1, source_target_pairs={{0,4},{4,0},{8,12},{12,8},{16,20},{20,16},{24,28},{28,24},{32,36},... | collective-permute-start | bytes 196616 | tf_op jit(solution)/shard_map/ppermute | solution.py:244
  13.7 6.0 %collective-permute-start.4 = (bf16[16,1024]{1,0:T(8,128)(2,1)S(1)}, bf16[16,1024]{1,0:T(8,128)(2,1)S(1)}, u32[]{:S(2)}, u32[]{:S(2)}) collective-permute-start(bf16[16,1024]{1,0:T(8,128)(2,1)S(1)} %core_sent.1), channel_id=1, source_target_pairs={{0,4},{4,0},{8,12},{12,8},{16,20},{20,16},{24,28},{28,24},{32,36},... | collective-permute-start | bytes 98312 | tf_op jit(solution)/shard_map/ppermute | solution.py:244
  18.3 5.5 %collective-permute-start.5 = (bf16[16,1024]{1,0:T(8,128)(2,1)S(1)}, bf16[16,1024]{1,0:T(8,128)(2,1)S(1)}, u32[]{:S(2)}, u32[]{:S(2)}) collective-permute-start(bf16[16,1024]{1,0:T(8,128)(2,1)S(1)} %far_sent.1), channel_id=1, source_target_pairs={{0,4},{4,0},{8,12},{12,8},{16,20},{20,16},{24,28},{28,24},{32,36},... | collective-permute-start | bytes 98312 | tf_op jit(solution)/shard_map/ppermute | solution.py:244
  20.6 6.5 %collective-permute-start.6 = (bf16[32,1024]{1,0:T(8,128)(2,1)S(1)}, bf16[32,1024]{1,0:T(8,128)(2,1)S(1)}, u32[]{:S(2)}, u32[]{:S(2)}) collective-permute-start(bf16[32,1024]{1,0:T(8,128)(2,1)S(1)} %get-tuple-element.86), channel_id=1, source_target_pairs={{0,8},{4,12},{8,0},{12,4},{16,24},{20,28},{24,16},{28,20},{32,40},... | collective-permute-start | bytes 196616 | tf_op jit(solution)/shard_map/ppermute | solution.py:244
  24.5 5.9 %collective-permute-start.7 = (bf16[32,1024]{1,0:T(8,128)(2,1)S(1)}, bf16[32,1024]{1,0:T(8,128)(2,1)S(1)}, u32[]{:S(2)}, u32[]{:S(2)}) collective-permute-start(bf16[32,1024]{1,0:T(8,128)(2,1)S(1)} %get-tuple-element.93), channel_id=1, source_target_pairs={{0,8},{4,12},{8,0},{12,4},{16,24},{20,28},{24,16},{28,20},{32,40},... | collective-permute-start | bytes 196616 | tf_op jit(solution)/shard_map/ppermute | solution.py:244
  27.9 4.4 %collective-permute-start.8 = (bf16[32,1024]{1,0:T(8,128)(2,1)S(1)}, bf16[32,1024]{1,0:T(8,128)(2,1)S(1)}, u32[]{:S(2)}, u32[]{:S(2)}) collective-permute-start(bf16[32,1024]{1,0:T(8,128)(2,1)S(1)} %get-tuple-element.96), channel_id=1, source_target_pairs={{0,16},{4,20},{8,24},{12,28},{16,0},{20,4},{24,8},{28,12},{32,48},... | collective-permute-start | bytes 196616 | tf_op jit(solution)/shard_map/ppermute | solution.py:244
  31.2 4.4 %collective-permute-start.9 = (bf16[32,1024]{1,0:T(8,128)(2,1)S(1)}, bf16[32,1024]{1,0:T(8,128)(2,1)S(1)}, u32[]{:S(2)}, u32[]{:S(2)}) collective-permute-start(bf16[32,1024]{1,0:T(8,128)(2,1)S(1)} %get-tuple-element.103), channel_id=1, source_target_pairs={{0,16},{4,20},{8,24},{12,28},{16,0},{20,4},{24,8},{28,12},{32,48},... | collective-permute-start | bytes 196616 | tf_op jit(solution)/shard_map/ppermute | solution.py:244
  33.0 5.5 %collective-permute-start.10 = (bf16[32,1024]{1,0:T(8,128)(2,1)S(1)}, bf16[32,1024]{1,0:T(8,128)(2,1)S(1)}, u32[]{:S(2)}, u32[]{:S(2)}) collective-permute-start(bf16[32,1024]{1,0:T(8,128)(2,1)S(1)} %get-tuple-element.106), channel_id=1, source_target_pairs={{0,32},{4,36},{8,40},{12,44},{16,48},{20,52},{24,56},{28,60},{32,0... | collective-permute-start | bytes 196616 | tf_op jit(solution)/shard_map/ppermute | solution.py:244
  36.3 5.3 %collective-permute-start.11 = (bf16[32,1024]{1,0:T(8,128)(2,1)S(1)}, bf16[32,1024]{1,0:T(8,128)(2,1)S(1)}, u32[]{:S(2)}, u32[]{:S(2)}) collective-permute-start(bf16[32,1024]{1,0:T(8,128)(2,1)S(1)} %get-tuple-element.113), channel_id=1, source_target_pairs={{0,32},{4,36},{8,40},{12,44},{16,48},{20,52},{24,56},{28,60},{32,0... | collective-permute-start | bytes 196616 | tf_op jit(solution)/shard_map/ppermute | solution.py:244
  39.3 5.1 %collective-permute-start.12 = (bf16[32,1024]{1,0:T(8,128)(2,1)S(1)}, bf16[32,1024]{1,0:T(8,128)(2,1)S(1)}, u32[]{:S(2)}, u32[]{:S(2)}) collective-permute-start(bf16[32,1024]{1,0:T(8,128)(2,1)S(1)} %get-tuple-element.116), channel_id=1, source_target_pairs={{0,64},{4,68},{8,72},{12,76},{16,80},{20,84},{24,88},{28,92},{32,9... | collective-permute-start | bytes 196616 | tf_op jit(solution)/shard_map/ppermute | solution.py:244
  42.4 6.2 %collective-permute-start.13 = (bf16[32,1024]{1,0:T(8,128)(2,1)S(1)}, bf16[32,1024]{1,0:T(8,128)(2,1)S(1)}, u32[]{:S(2)}, u32[]{:S(2)}) collective-permute-start(bf16[32,1024]{1,0:T(8,128)(2,1)S(1)} %get-tuple-element.123), channel_id=1, source_target_pairs={{0,64},{4,68},{8,72},{12,76},{16,80},{20,84},{24,88},{28,92},{32,9... | collective-permute-start | bytes 196616 | tf_op jit(solution)/shard_map/ppermute | solution.py:244
  45.2 6.0 %collective-permute-start.14 = (bf16[32,1024]{1,0:T(8,128)(2,1)S(1)}, bf16[32,1024]{1,0:T(8,128)(2,1)S(1)}, u32[]{:S(2)}, u32[]{:S(2)}) collective-permute-start(bf16[32,1024]{1,0:T(8,128)(2,1)S(1)} %get-tuple-element.126), channel_id=1, source_target_pairs={{0,128},{4,132},{8,136},{12,140},{16,144},{20,148},{24,152},{28,15... | collective-permute-start | bytes 196616 | tf_op jit(solution)/shard_map/ppermute | solution.py:244
  49.4 5.9 %collective-permute-start.15 = (bf16[32,1024]{1,0:T(8,128)(2,1)S(1)}, bf16[32,1024]{1,0:T(8,128)(2,1)S(1)}, u32[]{:S(2)}, u32[]{:S(2)}) collective-permute-start(bf16[32,1024]{1,0:T(8,128)(2,1)S(1)} %get-tuple-element.128), channel_id=1, source_target_pairs={{0,128},{4,132},{8,136},{12,140},{16,144},{20,148},{24,152},{28,15... | collective-permute-start | bytes 196616 | tf_op jit(solution)/shard_map/ppermute | solution.py:244
  51.7 4.0 %collective-permute-start.16 = (bf16[64,8,128]{2,1,0:T(8,128)(2,1)S(1)}, bf16[64,8,128]{2,1,0:T(8,128)(2,1)S(1)}, u32[]{:S(2)}, u32[]{:S(2)}) collective-permute-start(bf16[64,8,128]{2,1,0:T(8,128)(2,1)S(1)} %last.3), channel_id=1, source_target_pairs={{0,1},{1,0},{2,3},{3,2},{4,5},{5,4},{6,7},{7,6},{8,9},{9,8},{10,11... | collective-permute-start | bytes 393224 | tf_op jit(solution)/shard_map/ppermute | solution.py:248
